TPU v7x, 32 devices: a whole 2x2x4 slice. The times are simulated.
32 devices in a mesh: seq: 16 (over z, y, core), head: 2 (over x).
Axes of the slice: x: 2, y: 2, z: 4, core: 2. Of those that a mesh axis runs over, the one named last changes fastest.
Arguments:
- tokens: bfloat16 [6144, 3072], P('seq'), may hold values from -70 to 70
- survive: int32 [6144], P('seq'), may hold values from 0 to 1, as said below
- norm_gain: float32 [3072], replicated, may hold values from 0.3 to 3
- w_qkv: bfloat16 [3072, 3, 3072], P(None, None, 'head'), may hold values from -0.109375 to 0.109375
- qk_gain: float32 [2, 24, 128], P(None, 'head'), may hold values from 0.5 to 2
- w_out: bfloat16 [3072, 3072], P('head'), may hold values from -0.109375 to 0.109375
Outputs:
- update: bfloat16 [6144, 3072], P('seq', 'head')
Inputs may be any that keep to these rules, and one draw needn't show every extreme that they name: `survive`: exactly 3072 tokens run in all. The 384 positions of one sequence shard hold anywhere from none to all 384 running tokens; in every draw some shard holds all 384 and some shard none.
All inputs are finite; a program needn't handle non-finite values.
Results may differ from a plain program's by a relative error of at most 0.015.
Values may be sent and summed in bfloat16 or wider, within the bound.
No kernel may reach another device: no remote copies, remote signals or barrier semaphores. Data moves between devices by JAX's collectives and lax.ppermute only.
A program may use at most 128 MiB of HBM per device.

v0:
```python
import math

import jax
import jax.numpy as jnp
from jax import lax
from jax.sharding import PartitionSpec as P

epsilon = 1e-06
key_limit = 2048


def layer_norm(values, gain):
    center = values - jnp.mean(values, axis=-1, keepdims=True)
    spread = jnp.mean(center * center, axis=-1, keepdims=True)
    return center * lax.rsqrt(spread + epsilon) * gain


def project(source_tokens, norm_gain, w_qkv, qk_gain):
    width = source_tokens.shape[1]
    count_rows = source_tokens.shape[0]
    heads_here = qk_gain.shape[1]
    head_size = qk_gain.shape[2]
    inner_here = heads_here * head_size
    normed = layer_norm(source_tokens.astype(jnp.float32), norm_gain).astype(jnp.bfloat16)
    projected_output = jnp.dot(
        normed, w_qkv.reshape(width, 3 * inner_here), preferred_element_type=jnp.float32
    )
    query_rows = projected_output[:, :inner_here].reshape(count_rows, heads_here, head_size)
    running_key_rows = projected_output[:, inner_here : 2 * inner_here].reshape(
        count_rows, heads_here, head_size
    )
    query_rows = layer_norm(query_rows, qk_gain[0]).astype(jnp.bfloat16)
    running_key_rows = (
        layer_norm(running_key_rows, qk_gain[1])
        .astype(jnp.bfloat16)
        .reshape(count_rows, inner_here)
    )
    running_value_rows = projected_output[:, 2 * inner_here :].astype(jnp.bfloat16)
    return (query_rows, running_key_rows, running_value_rows)


def attend(query_rows, running_key_rows, running_value_rows, key_live):
    count_rows, heads_here, head_size = query_rows.shape
    score_scale = 1.0 / math.sqrt(head_size)
    shard_keys = running_key_rows.shape[0]

    def one_block(running, block_data):
        numerator, denominator = running
        block_keys, block_values, block_live = block_data
        width_keys = block_keys.shape[0]
        scores = (
            jnp.einsum(
                "qhd,khd->hqk",
                query_rows,
                block_keys.reshape(width_keys, heads_here, head_size),
                preferred_element_type=jnp.float32,
            )
            * score_scale
        )
        weights = jnp.exp(scores) * block_live.astype(jnp.float32)[None, None, :]
        denominator = denominator + jnp.sum(weights, axis=-1)
        numerator = numerator + jnp.einsum(
            "hqk,khd->qhd",
            weights.astype(jnp.bfloat16),
            block_values.reshape(width_keys, heads_here, head_size),
            preferred_element_type=jnp.float32,
        )
        return ((numerator, denominator), None)

    initial = (
        jnp.zeros(query_rows.shape, jnp.float32),
        jnp.zeros((heads_here, count_rows), jnp.float32),
    )
    running = initial
    piece_keys = lax.all_gather(running_key_rows, "seq", axis=0, tiled=True)
    piece_values = lax.all_gather(running_value_rows, "seq", axis=0, tiled=True)
    piece_live = lax.all_gather(key_live, "seq", axis=0, tiled=True)
    length = piece_keys.shape[0]
    shards_in = length // shard_keys
    most_shards = max(key_limit // shard_keys, 1)
    power_shards = 1 << most_shards.bit_length() - 1
    group_size = math.gcd(shards_in, power_shards)
    block_len = group_size * shard_keys
    blocks = length // block_len
    stacked = (
        piece_keys.reshape(blocks, block_len, piece_keys.shape[1]),
        piece_values.reshape(blocks, block_len, piece_values.shape[1]),
        piece_live.reshape(blocks, block_len),
    )
    running, unused = lax.scan(one_block, running, stacked)
    numerator, denominator = running
    attended_output = numerator / jnp.transpose(denominator)[:, :, None]
    return attended_output.astype(jnp.bfloat16).reshape(count_rows, heads_here * head_size)


def deal_plan(survive, counts_all, alive_count):
    positions = survive.shape[0]
    shards = lax.axis_size("seq")
    capacity = positions // shards
    kept_rows = positions // 2
    my_index = lax.axis_index("seq")
    starts = jnp.cumsum(counts_all) - counts_all
    offset = lax.dynamic_index_in_dim(starts, my_index, 0, keepdims=False)
    target = jnp.arange(shards, dtype=jnp.int32)[:, None]
    slot_index = jnp.arange(capacity, dtype=jnp.int32)[None, :]
    first_slot = (offset + shards - 1 - target) // shards
    global_rank = target + shards * (first_slot + slot_index)
    local_rank = global_rank - offset
    occupied = local_rank < alive_count
    local_order = jnp.argsort(1 - survive, stable=True)
    source_pos = local_order[jnp.clip(local_rank, 0, positions - 1)]
    first_from = (starts + shards - 1 - my_index) // shards
    last_from = (starts + counts_all + shards - 1 - my_index) // shards
    per_source = last_from - first_from
    usable = (slot_index < per_source[:, None]).reshape(shards * capacity)
    chosen = jnp.argsort(jnp.where(usable, 0, 1), stable=True)[:kept_rows]
    return (occupied, source_pos, chosen)


def place_back(returned, occupied, source_pos, positions, width_share):
    total_slots = occupied.shape[0] * occupied.shape[1]
    drop_pos = jnp.where(occupied, source_pos, positions).reshape(total_slots)
    return (
        jnp.zeros((positions, width_share), jnp.bfloat16)
        .at[drop_pos]
        .set(returned.reshape(total_slots, width_share), mode="drop")
    )


def per_device(tokens, survive, norm_gain, w_qkv, qk_gain, w_out):
    positions = tokens.shape[0]
    shards = lax.axis_size("seq")
    capacity = positions // shards
    kept_rows = positions // 2
    alive_count = jnp.sum(survive)
    counts_all = lax.all_gather(alive_count.reshape(1), "seq", axis=0, tiled=True)
    occupied, source_pos, chosen = deal_plan(survive, counts_all, alive_count)
    key_live = jnp.ones((kept_rows,), jnp.bfloat16)
    outgoing = jnp.where(occupied[:, :, None], tokens[source_pos], jnp.zeros((), tokens.dtype))
    arrived = lax.all_to_all(outgoing, "seq", split_axis=0, concat_axis=0, tiled=True)
    source_tokens = arrived.reshape(shards * capacity, tokens.shape[1])[chosen]
    query_rows, running_key_rows, running_value_rows = project(
        source_tokens, norm_gain, w_qkv, qk_gain
    )
    attended_output = attend(query_rows, running_key_rows, running_value_rows, key_live)
    branch_terms = jnp.dot(attended_output, w_out, preferred_element_type=jnp.float32)
    head_share = lax.psum_scatter(
        branch_terms.astype(jnp.bfloat16), "head", scatter_dimension=1, tiled=True
    ).astype(jnp.float32)
    width_share = head_share.shape[1]
    placed = (
        jnp.zeros((shards * capacity, width_share), jnp.bfloat16)
        .at[chosen]
        .set(head_share.astype(jnp.bfloat16))
    )
    returned = lax.all_to_all(
        placed.reshape(shards, capacity, width_share),
        "seq",
        split_axis=0,
        concat_axis=0,
        tiled=True,
    )
    update = place_back(returned, occupied, source_pos, positions, width_share)
    return update


def solution(mesh):
    placed = (
        P("seq", None),
        P("seq"),
        P(),
        P(None, None, "head"),
        P(None, "head", None),
        P("head", None),
    )
    return jax.shard_map(
        per_device, mesh=mesh, in_specs=placed, out_specs=P("seq", "head"), check_vma=False
    )
```

profile of v0, /device:TPU:0, one launch (start us, length us, event | category | flops | bytes accessed | tf_op | source)
XLA Modules:
  0.0 433.2 jit_solution(3832122362893557765)
XLA Ops:
  6.5 1.5 fusion.29
  8.0 1.2 dynamic-slice
  9.3 1.4 dynamic-update-slice
  10.6 13.7 %all-reduce = s32[16]{0:T(128)S(1)} all-reduce(s32[16]{0:T(128)S(1)} %dynamic-update-slice), channel_id=1, replica_groups=mesh['seq'=16,'head'=2] {'seq'}, use_global_device_ids=true, to_apply=%add | all-reduce | flops 16 | bytes 128
  24.6 0.6 dynamic_slice.19
  25.8 1.2 subtract_compare_fusion
  27.0 0.6 compare_select_fusion.1
  27.7 3.8 sort.34
  31.5 2.8 gather_fusion
  34.5 3.6 gather_fusion.1
  38.1 3.4 broadcast_select_fusion
  41.5 3.7 all-to-all-start
  45.5 36.7 %copy.14 = bf16[3072,3,1536]{0,2,1:T(8,128)(2,1)} copy(bf16[3072,3,1536]{2,0,1:T(8,128)(2,1)} %param.11) | data formatting | bytes 56623104 | tf_op args[3]
  82.2 3.8 sort.35
  86.0 0.6 copy-done.9
  86.5 4.3 %all-to-all-done = bf16[16,24,3072]{2,1,0:T(8,128)(2,1)S(1)} async-done(((bf16[16,24,3072]{2,1,0:T(8,128)(2,1)}), bf16[16,24,3072]{2,1,0:T(8,128)(2,1)S(1)}, u32[]{:S(2)}, u32[]{:S(2)}) %all-to-all-start) | async-done | bytes 2359328 | tf_op jit(solution)/shard_map/all_to_all | solution.py:140
  90.9 1.3 gather_fusion.2
  92.9 16.0 %fusion.10 = f32[192,4608]{1,0:T(8,128)} fusion(bf16[3072,4608]{0,1:T(8,128)(2,1)} %bitcast.83, bf16[192,3072]{1,0:T(8,128)(2,1)S(1)} %gather_fusion.2, f32[3072]{0:T(1024)S(1)} %copy-done.10, f32[192]{0:T(256)S(1)} %add_rsqrt_fusion.2, f32[192]{0:T(256)S(1)} %broadcast_multiply_fusion.2), kind=kOutput, calls=%fused_computation.28 | convolution fusion | flops 5438767104 | bytes 33043968 | tf_op jit(solution)/shard_map/dot_general | solution.py:25
  108.9 2.2 slice.37
  111.2 1.2 slice-done
  113.1 0.9 multiply_reduce_fusion.1
  115.0 1.0 copy-done.3
  116.0 1.7 fusion.27
  118.0 1.4 reshape.331
  119.4 1.9 reduce_sum.79
  121.3 2.4 multiply_reduce_fusion
  123.8 1.0 multiply_convert_fusion
  124.9 75.4 %all-gather.3.cloned.1.call-done = bf16[3072,1536]{1,0:T(8,128)(2,1)} async-done(((bf16[192,1536]{1,0:T(8,128)(2,1)}), bf16[3072,1536]{1,0:T(8,128)(2,1)}) %all-gather.3.cloned.1.call-update) | async-done | bytes 9437200 | tf_op jit(solution)/shard_map/all_gather | solution.py:76
  200.3 81.9 %all-gather.5.cloned.1.call-done = bf16[3072,1536]{1,0:T(8,128)(2,1)} async-done(((bf16[192,1536]{1,0:T(8,128)(2,1)}), bf16[3072,1536]{1,0:T(8,128)(2,1)}) %all-gather.5.cloned.1.call-update) | async-done | bytes 9437200 | tf_op jit(solution)/shard_map/all_gather | solution.py:75
  282.2 80.1 %while.14 = (s32[]{:T(128)}, f32[192,12,128]{2,0,1:T(8,128)S(1)}, f32[12,192]{1,0:T(8,128)S(1)}, bf16[2,1536,1536]{2,1,0:T(8,128)(2,1)}, bf16[2,1536,1536]{2,1,0...) while((s32[]{:T(128)}, f32[192,12,128]{2,0,1:T(8,128)S(1)}, ...), condition=%wide.region_12.13_spmd.clone, body=%wide.region_10.12_spmd.clone.sunk | while | flops 1826687232 | bytes 78483560 | solution.py:90
  282.2 8.0 %constant_dynamic-slice_fusion.3 = (bf16[1,1536,1536]{2,1,0:T(8,128)(2,1)}, bf16[1,1536,1536]{2,1,0:T(8,128)(2,1)}) fusion(bf16[2,1536,1536]{2,1,0:T(8,128)(2,1)} %get-tuple-element.183, s32[]{:T(128)S(6)} %copy.48, bf16[2,1536,1536]{2,1,0:T(8,128)(2,1)} %get-tuple-element.182), kind=kLoop, calls=%fused_computation.13.clone.1 | loop fusion | bytes 18874372 | tf_op jit(solution)/shard_map/while/body/jit(dynamic_index_in_dim)/dynamic_slice | solution.py:90
  290.2 6.7 %copy.42 = bf16[1,1536,1536]{1,2,0:T(8,128)(2,1)} copy(bf16[1,1536,1536]{2,1,0:T(8,128)(2,1)} %get-tuple-element.159) | data formatting | bytes 9437184 | tf_op jit(solution)/shard_map/while/body/jit(dynamic_index_in_dim)/dynamic_slice | solution.py:90
  296.9 6.7 %copy.43 = bf16[1,1536,1536]{1,2,0:T(8,128)(2,1)} copy(bf16[1,1536,1536]{2,1,0:T(8,128)(2,1)} %get-tuple-element.160) | data formatting | bytes 9437184 | tf_op jit(solution)/shard_map/while/body/jit(dynamic_index_in_dim)/dynamic_slice | solution.py:90
  303.5 9.9 %bitcast_reduce_fusion.2 = (f32[12,192]{1,0:T(8,128)S(1)}, f32[12,1536,192]{1,2,0:T(8,128)}) fusion(bf16[192,12,128]{2,0,1:T(8,128)(2,1)S(1)} %get-tuple-element.184, bf16[1536,12,128]{0,2,1:T(8,128)(2,1)} %bitcast.78), kind=kOutput, calls=%fused_computation.5.clone.1 | convolution fusion | flops 913045248 | bytes 19473408 | tf_op jit(solution)/shard_map/while/body/eval_jaxpr/qhd,khd->hqk/dot_general | solution.py:52
  313.4 8.8 %fusion.44 = f32[192,12,128]{2,0,1:T(8,128)S(1)} fusion(bf16[1536,12,128]{0,2,1:T(8,128)(2,1)} %bitcast.79, f32[12,1536,192]{1,2,0:T(8,128)} %get-tuple-element.161, f32[192,12,128]{2,0,1:T(8,128)S(1)} %get-tuple-element.172, pred[]{:T(512)S(6)} %compare.24), kind=kOutput, calls=%fused_computation.11.clone.1 | convolution fusion | flops 913637376 | bytes 21233664 | tf_op jit(solution)/shard_map/while/body/eval_jaxpr/hqk,khd->qhd/dot_general | solution.py:62
  322.2 8.0 %constant_dynamic-slice_fusion.3 = (bf16[1,1536,1536]{2,1,0:T(8,128)(2,1)}, bf16[1,1536,1536]{2,1,0:T(8,128)(2,1)}) fusion(bf16[2,1536,1536]{2,1,0:T(8,128)(2,1)} %get-tuple-element.183, s32[]{:T(128)S(6)} %copy.48, bf16[2,1536,1536]{2,1,0:T(8,128)(2,1)} %get-tuple-element.182), kind=kLoop, calls=%fused_computation.13.clone.1 | loop fusion | bytes 18874372 | tf_op jit(solution)/shard_map/while/body/jit(dynamic_index_in_dim)/dynamic_slice | solution.py:90
  330.2 6.7 %copy.42 = bf16[1,1536,1536]{1,2,0:T(8,128)(2,1)} copy(bf16[1,1536,1536]{2,1,0:T(8,128)(2,1)} %get-tuple-element.159) | data formatting | bytes 9437184 | tf_op jit(solution)/shard_map/while/body/jit(dynamic_index_in_dim)/dynamic_slice | solution.py:90
  336.9 6.7 %copy.43 = bf16[1,1536,1536]{1,2,0:T(8,128)(2,1)} copy(bf16[1,1536,1536]{2,1,0:T(8,128)(2,1)} %get-tuple-element.160) | data formatting | bytes 9437184 | tf_op jit(solution)/shard_map/while/body/jit(dynamic_index_in_dim)/dynamic_slice | solution.py:90
  343.6 9.9 %bitcast_reduce_fusion.2 = (f32[12,192]{1,0:T(8,128)S(1)}, f32[12,1536,192]{1,2,0:T(8,128)}) fusion(bf16[192,12,128]{2,0,1:T(8,128)(2,1)S(1)} %get-tuple-element.184, bf16[1536,12,128]{0,2,1:T(8,128)(2,1)} %bitcast.78), kind=kOutput, calls=%fused_computation.5.clone.1 | convolution fusion | flops 913045248 | bytes 19473408 | tf_op jit(solution)/shard_map/while/body/eval_jaxpr/qhd,khd->hqk/dot_general | solution.py:52
  353.4 8.8 %fusion.44 = f32[192,12,128]{2,0,1:T(8,128)S(1)} fusion(bf16[1536,12,128]{0,2,1:T(8,128)(2,1)} %bitcast.79, f32[12,1536,192]{1,2,0:T(8,128)} %get-tuple-element.161, f32[192,12,128]{2,0,1:T(8,128)S(1)} %get-tuple-element.172, pred[]{:T(512)S(6)} %compare.24), kind=kOutput, calls=%fused_computation.11.clone.1 | convolution fusion | flops 913637376 | bytes 21233664 | tf_op jit(solution)/shard_map/while/body/eval_jaxpr/hqk,khd->qhd/dot_general | solution.py:62
  362.3 6.8 %convolution_convert_fusion = bf16[192,3072]{1,0:T(8,128)(2,1)} fusion(bf16[1536,3072]{1,0:T(8,128)(2,1)} %param.13, f32[192,12,128]{2,0,1:T(8,128)S(1)} %get-tuple-element.65, f32[192,12]{0,1:T(8,128)S(1)} %bitcast.88), kind=kOutput, calls=%fused_computation.16 | convolution fusion | flops 1813118976 | bytes 11805696 | tf_op jit(solution)/shard_map/dot_general | solution.py:146
  369.1 20.0 %reduce-scatter.2.cloned.1.call-done = bf16[192,1536]{1,0:T(8,128)(2,1)} async-done(((bf16[192,3072]{1,0:T(8,128)(2,1)}), bf16[192,1536]{1,0:T(8,128)(2,1)}) %reduce-scatter.2.cloned.1.call-update) | async-done | bytes 589840 | tf_op jit(solution)/shard_map/reduce_scatter | solution.py:147
  389.1 3.2 scatter_custom_fusion
  392.3 5.8 %all-to-all-start.1 = ((bf16[16,24,1536]{2,1,0:T(8,128)(2,1)}), bf16[16,24,1536]{2,1,0:T(8,128)(2,1)S(1)}, u32[]{:S(2)}, u32[]{:S(2)}) async-start(bf16[16,24,1536]{2,1,0:T(8,128)(2,1)} %bitcast.12), calls=%async_computation.2 | async-start | bytes 2359296 | tf_op jit(solution)/shard_map/all_to_all | solution.py:156
  398.1 1.8 broadcast_select_fusion.1
  400.0 0.8 reshape.338
  400.8 22.4 %all-to-all-done.1 = bf16[16,24,1536]{2,1,0:T(8,128)(2,1)S(1)} async-done(((bf16[16,24,1536]{2,1,0:T(8,128)(2,1)}), bf16[16,24,1536]{2,1,0:T(8,128)(2,1)S(1)}, u32[]{:S(2)}, u32[]{:S(2)}) %all-to-all-start.1) | async-done | bytes 1179680 | tf_op jit(solution)/shard_map/all_to_all | solution.py:156
  423.2 3.5 scatter_custom_fusion.1
  (67 shorter events, 3.8 us)
Async XLA Ops:
  6.5 28.0 %copy-start = (bf16[384,3072]{1,0:T(8,128)(2,1)S(1)}, bf16[384,3072]{1,0:T(8,128)(2,1)}, u32[]{:S(2)}) copy-start(bf16[384,3072]{1,0:T(8,128)(2,1)} %param.8) | copy-start | bytes 7077892
  25.8 5.8 %copy-start.7 = (s32[16]{0:T(128)}, s32[16]{0:T(128)S(1)}, u32[]{:S(2)}) copy-start(s32[16]{0:T(128)S(1)} %and_select_fusion.2) | copy-start | bytes 196
  34.3 3.8 copy-start.4
  41.5 49.3 %all-to-all-start = ((bf16[16,24,3072]{2,1,0:T(8,128)(2,1)}), bf16[16,24,3072]{2,1,0:T(8,128)(2,1)S(1)}, u32[]{:S(2)}, u32[]{:S(2)}) async-start(bf16[16,24,3072]{2,1,0:T(8,128)(2,1)} %broadcast_select_fusion), calls=%async_computation | async-start | bytes 4718592 | tf_op jit(solution)/shard_map/all_to_all | solution.py:140
  45.3 155.0 %all-gather.3.cloned.1.call-start = ((), (), s32[]{:S(2)}) async-start(), calls=%async_computation.3 | async-start | bytes 10027008 | tf_op jit(solution)/shard_map/all_gather | solution.py:76
  86.0 0.6 copy-start.9
  92.2 0.7 copy-start.10
  108.9 2.2 copy-start.6
  111.1 1.3 slice-start
  111.1 171.0 %all-gather.5.cloned.1.call-start = ((), (), s32[]{:S(2)}) async-start(), calls=%async_computation.4 | async-start | bytes 10027008 | tf_op jit(solution)/shard_map/all_gather | solution.py:75
  114.0 2.0 copy-start.3
  117.7 271.4 %reduce-scatter.2.cloned.1.call-start = ((), (), s32[]{:S(2)}) async-start(), calls=%async_computation.5 | async-start | bytes 1769472 | tf_op jit(solution)/shard_map/reduce_scatter | solution.py:147
  121.3 2.5 copy-start.2
  369.1 29.0 %copy-start.5 = (s32[384]{0:T(512)S(1)}, s32[384]{0:T(512)}, u32[]{:S(2)}) copy-start(s32[384]{0:T(512)} %copy-done.4) | copy-start | bytes 4612
  369.1 29.1 %copy-start.8 = (s32[16]{0:T(128)S(1)}, s32[16]{0:T(128)}, u32[]{:S(2)}) copy-start(s32[16]{0:T(128)} %copy-done.7) | copy-start | bytes 196
  392.3 34.4 %copy-start.1 = (bf16[384,3072]{1,0:T(8,128)(2,1)S(1)}, bf16[384,3072]{1,0:T(8,128)(2,1)}, u32[]{:S(2)}) copy-start(bf16[384,3072]{1,0:T(8,128)(2,1)} %param.8) | copy-start | bytes 7077892
  392.3 30.9 %all-to-all-start.1 = ((bf16[16,24,1536]{2,1,0:T(8,128)(2,1)}), bf16[16,24,1536]{2,1,0:T(8,128)(2,1)S(1)}, u32[]{:S(2)}, u32[]{:S(2)}) async-start(bf16[16,24,1536]{2,1,0:T(8,128)(2,1)} %bitcast.12), calls=%async_computation.2 | async-start | bytes 2359296 | tf_op jit(solution)/shard_map/all_to_all | solution.py:156
Sparse Core Ops, SparseCore 0:
  111.2 88.9 all-gather.2
  202.6 79.5 all-gather.4
  369.2 19.8 reduce-scatter.1
where the time goes:
time: 437 us; the launch traced here: 433 us
  waiting for transfers between devices  204 us (47%)
  local copies, waits for them, and re-layouts  106 us (24%)
  matrix products  60.1 us (14%)
  other arithmetic  25.6 us (6%)
  between operations  14 us (3%)
  blocking collectives  13.7 us (3%)
  starting transfers between devices  9.79 us (2%)
    all_gather x1, waiting for transfers between devices, attend(): piece_keys = lax.all_gather(running_key_rows, 'seq', axis=0, tiled=True)  81.9 us
    all_gather x1, waiting for transfers between devices, attend(): piece_values = lax.all_gather(running_value_rows, 'seq', axis=0, tiled=True)  75.4 us
    dynamic_slice x6, local copies, waits for them, and re-layouts, attend(): running, unused = lax.scan(one_block, running, stacked)  42.7 us
    unnamed x29, local copies, waits for them, and re-layouts  41.1 us
    all_to_all x1, waiting for transfers between devices, per_device(): lax.all_to_all(placed.reshape(shards, capacity, width_share), 'seq', spli...  22.4 us
    reduce_scatter x1, waiting for transfers between devices, per_device(): lax.psum_scatter(branch_terms.astype(jnp.bfloat16), 'head', scatter_dimen...  20 us
    dot_general x2, matrix products, one_block(): jnp.einsum('qhd,khd->hqk', query_rows, block_keys.reshape(width_keys, hea...  19.7 us
    dot_general x2, matrix products, one_block(): jnp.einsum('hqk,khd->qhd', weights.astype(jnp.bfloat16), block_values.res...  17.6 us
  transfers between devices with their start and end apart: 5, of which 5 were waited for; matrix products, arithmetic and copies ran while one was open for 13% of the time, Pallas kernels for 0%

commit v1 on v0

v1 whole, which is shorter than its diff:
```python
import functools
import math

import jax
import jax.numpy as jnp
from jax import lax
from jax.experimental import pallas as pl
from jax.experimental.pallas import tpu as pltpu
from jax.sharding import PartitionSpec as P

epsilon = 1e-06
mib = 1 << 20
f32 = jnp.float32
bf16 = jnp.bfloat16


def layer_norm(values, gain):
    center = values - jnp.mean(values, axis=-1, keepdims=True)
    spread = jnp.mean(center * center, axis=-1, keepdims=True)
    return center * lax.rsqrt(spread + epsilon) * gain


def cost(flops, bytes_accessed, exps=0):
    return pl.CostEstimate(
        flops=int(flops), bytes_accessed=int(bytes_accessed), transcendentals=int(exps)
    )


def pack_body(row_ref, col_ref, tokens_ref, gain_ref, normed_ref, back_ref, *, rows):
    positions = tokens_ref.shape[0]
    step = pl.program_id(0)
    first = lax.broadcasted_iota(jnp.int32, (positions, positions), 0)
    second = lax.broadcasted_iota(jnp.int32, (positions, positions), 1)
    live_row = jnp.broadcast_to(row_ref[...].astype(f32), (8, positions))
    upper = (first <= second).astype(f32).astype(bf16)
    rank_row = jnp.dot(live_row.astype(bf16), upper, preferred_element_type=f32)[:1]
    target = jnp.where(live_row[:1] > 0.5, rank_row - 1.0, -1.0).astype(jnp.int32)
    slots = lax.broadcasted_iota(jnp.int32, (rows, positions), 0) + step * rows
    chosen = (slots == target).astype(f32).astype(bf16)
    packed = jnp.dot(chosen, tokens_ref[...], preferred_element_type=f32)
    normed_ref[...] = layer_norm(packed, gain_ref[...]).astype(bf16)

    @pl.when(step == 0)
    def _():
        live_col = jnp.broadcast_to(col_ref[...].astype(f32), (positions, 128))
        lower = (first >= second).astype(f32).astype(bf16)
        rank_col = jnp.dot(lower, live_col.astype(bf16), preferred_element_type=f32)[:, :1]
        home = jnp.where(live_col[:, :1] > 0.5, rank_col - 1.0, -1.0).astype(jnp.int32)
        back_ref[...] = (second == home).astype(f32).astype(bf16)


def pack(tokens, survive, norm_gain):
    positions, width = tokens.shape
    rows = 128 if positions % 128 == 0 else positions
    whole = lambda i: (0, 0)
    return pl.pallas_call(
        functools.partial(pack_body, rows=rows),
        grid=(positions // rows,),
        in_specs=[
            pl.BlockSpec((1, positions), whole),
            pl.BlockSpec((positions, 1), whole),
            pl.BlockSpec((positions, width), whole),
            pl.BlockSpec((1, width), whole),
        ],
        out_specs=[
            pl.BlockSpec((rows, width), lambda i: (i, 0)),
            pl.BlockSpec((positions, positions), whole),
        ],
        out_shape=[
            jax.ShapeDtypeStruct((positions, width), bf16),
            jax.ShapeDtypeStruct((positions, positions), bf16),
        ],
        compiler_params=pltpu.CompilerParams(vmem_limit_bytes=32 * mib),
        cost_estimate=cost(2 * positions * positions * width, 4 * positions * width),
        name="pack",
    )(
        survive.reshape(1, positions),
        survive.reshape(positions, 1),
        tokens,
        norm_gain.reshape(1, width),
    )


def project_body(normed_ref, weight_ref, gain_ref, keyval_ref, query_ref, *, first_head, tile_heads):
    size = query_ref.shape[2]
    tile, kind = pl.program_id(0), pl.program_id(1)
    result = jnp.dot(normed_ref[...], weight_ref[0], preferred_element_type=f32)
    parts = [result[:, i * size : (i + 1) * size] for i in range(tile_heads)]

    def gain(which, i):
        return gain_ref[which, pl.ds(first_head + tile * tile_heads + i, 1), :]

    @pl.when(kind == 0)
    def _():
        for i, part in enumerate(parts):
            keyval_ref[i, :, :size] = layer_norm(part, gain(1, i)).astype(bf16)

    @pl.when(kind == 1)
    def _():
        for i, part in enumerate(parts):
            keyval_ref[i, :, size:] = part.astype(bf16)

    @pl.when(kind == 2)
    def _():
        for i, part in enumerate(parts):
            query_ref[i] = layer_norm(part, gain(0, i)).astype(bf16)


def project(normed, weights, qk_gain, chunk, groups):
    rows, width = normed.shape
    size = qk_gain.shape[2]
    tile_heads = 2 if groups % 2 == 0 else 1
    tiles = groups // tile_heads
    columns = tile_heads * size
    return pl.pallas_call(
        functools.partial(project_body, first_head=chunk * groups, tile_heads=tile_heads),
        grid=(tiles, 3),
        in_specs=[
            pl.BlockSpec((rows, width), lambda n, t: (0, 0)),
            pl.BlockSpec((1, width, columns), lambda n, t: ((t + 1) % 3, 0, chunk * tiles + n)),
            pl.BlockSpec(qk_gain.shape, lambda n, t: (0, 0, 0)),
        ],
        out_specs=[
            pl.BlockSpec((tile_heads, rows, 2 * size), lambda n, t: (n, 0, 0)),
            pl.BlockSpec((tile_heads, rows, size), lambda n, t: (n, 0, 0)),
        ],
        out_shape=[
            jax.ShapeDtypeStruct((groups, rows, 2 * size), bf16),
            jax.ShapeDtypeStruct((groups, rows, size), bf16),
        ],
        compiler_params=pltpu.CompilerParams(vmem_limit_bytes=32 * mib),
        cost_estimate=cost(
            2 * rows * width * 3 * groups * size, 6 * width * groups * size + 2 * rows * width
        ),
        name="project",
    )(normed, weights, qk_gain)


def attend_body(counts_ref, query_ref, *refs, sources, key_room, query_rows, key_cols):
    keyval_refs = refs[:sources]
    out_ref, keys, values, queries, results = refs[sources:]
    groups, rows, size = query_ref.shape
    piece = 128 if rows % 128 == 0 else rows
    scale = math.log2(math.e) / math.sqrt(size)
    align = lambda count: pl.multiple_of((count + 15) // 16 * 16, 16)
    line = lax.broadcasted_iota(jnp.int32, (piece, size), 0)

    def keep(source, block, offset, count):
        for part in range(rows // piece):

            @pl.when(part * piece < count)
            def _():
                here = pl.ds(pl.multiple_of(offset + part * piece, 16), piece)
                there = pl.ds(part * piece, piece)
                keys[here, :] = source[block, there, :size]
                values[here, :size] = source[block, there, size:]
                live = (line + part * piece < count).astype(f32).astype(bf16)
                values[here, size:] = live

        return pl.multiple_of(offset + align(count), 16)

    offset = jnp.int32(0)
    index = 0
    for source in keyval_refs:
        for block in range(source.shape[0]):
            offset = keep(source, block, offset, counts_ref[index])
            index += 1
    total_blocks = index

    def clear(step, carry):
        here = pl.ds(pl.multiple_of(offset + step * 16, 16), 16)
        keys[here, :] = jnp.zeros((16, size), bf16)
        values[here, :] = jnp.zeros((16, 2 * size), bf16)
        return carry

    lax.fori_loop(0, (key_room - offset) // 16, clear, 0)

    starts = []
    start = jnp.int32(0)
    for block in range(groups):
        count = counts_ref[total_blocks + block]
        starts.append(start)
        for part in range(rows // piece):

            @pl.when(part * piece < count)
            def _():
                here = pl.ds(pl.multiple_of(start + part * piece, 16), piece)
                queries[here, :] = query_ref[block, part * piece : (part + 1) * piece, :]

        start = pl.multiple_of(start + align(count), 16)

    def one_tile(tile, carry):
        here = pl.ds(pl.multiple_of(tile * query_rows, query_rows), query_rows)
        query = queries[here, :]
        total = jnp.zeros((query_rows, 2 * size), f32)
        for low in range(0, key_room, key_cols):
            high = min(low + key_cols, key_room)
            scores = lax.dot_general(
                query, keys[low:high, :], (((1,), (1,)), ((), ())), preferred_element_type=f32
            )
            weights = jnp.exp2(scores * scale).astype(bf16)
            total += jnp.dot(weights, values[low:high, :], preferred_element_type=f32)
        results[here, :] = (total[:, :size] / total[:, size:]).astype(bf16)
        return carry

    lax.fori_loop(0, (start + query_rows - 1) // query_rows, one_tile, 0)

    for block in range(groups):
        count = counts_ref[total_blocks + block]
        for part in range(rows // piece):
            here = pl.ds(pl.multiple_of(starts[block] + part * piece, 16), piece)
            found = results[here, :]
            live = line + part * piece < count
            out_ref[block, part * piece : (part + 1) * piece, :] = jnp.where(
                live, found.astype(f32), 0.0
            ).astype(bf16)


def attend(counts, query, keyvals, shards):
    groups, rows, size = query.shape
    running = shards * rows // 2
    key_room = -(-(running + 16 * shards) // 256) * 256
    query_rows = 256
    query_room = -(-groups * rows // query_rows) * query_rows + rows
    sources = len(keyvals)
    return pl.pallas_call(
        functools.partial(
            attend_body,
            sources=sources,
            key_room=key_room,
            query_rows=query_rows,
            key_cols=512,
        ),
        in_specs=[pl.BlockSpec(memory_space=pltpu.SMEM)]
        + [pl.BlockSpec(memory_space=pltpu.VMEM)] * (1 + sources),
        out_specs=pl.BlockSpec(memory_space=pltpu.VMEM),
        out_shape=jax.ShapeDtypeStruct((groups, rows, size), bf16),
        scratch_shapes=[
            pltpu.VMEM((key_room + rows, size), bf16),
            pltpu.VMEM((key_room + rows, 2 * size), bf16),
            pltpu.VMEM((query_room, size), bf16),
            pltpu.VMEM((query_room, size), bf16),
        ],
        compiler_params=pltpu.CompilerParams(vmem_limit_bytes=40 * mib),
        cost_estimate=cost(
            8 * groups * rows // 2 * running * size,
            4 * shards * rows * size,
            groups * rows // 2 * running,
        ),
        name="attend",
    )(counts, query, *keyvals)


def finish_body(place_ref, *refs, others, has_sum, last):
    refs = list(refs)
    out_ref = refs.pop()
    step = pl.program_id(0)
    total = refs.pop(0)[...] if has_sum else None

    def add(total, attended_ref, weight):
        groups = attended_ref.shape[0]
        wide = jnp.concatenate([attended_ref[g] for g in range(groups)], axis=-1)
        term = jnp.dot(wide, weight, preferred_element_type=f32)
        return term if total is None else total + term

    total = add(total, refs[0], refs[1][...])
    for m in range(others):
        attended_ref, near_ref, far_ref = refs[2 + 3 * m : 5 + 3 * m]
        total = add(total, attended_ref, jnp.where(step == 0, near_ref[...], far_ref[...]))
    if last:
        rounded = total.astype(bf16)
        out_ref[...] = jnp.dot(refs[-1][...], rounded, preferred_element_type=f32).astype(bf16)
    else:
        out_ref[...] = total


def column_split(out_width):
    return 2 if out_width % 256 == 0 else 1


def finish(place, total, attended, w_out, other_attended, other_weights, back, chunk, out_width):
    groups, rows, size = attended.shape
    split = column_split(out_width)
    half = out_width // split
    depth = groups * size
    mine = lambda i, place: (0, lax.bitwise_xor(place[0], i))
    block_a = pl.BlockSpec((groups, rows, size), lambda i, place: (0, 0, 0))
    block_w = pl.BlockSpec((depth, half), lambda i, place: (chunk, 0))
    specs, operands = [], []
    if total is not None:
        specs.append(pl.BlockSpec((rows, half), mine))
        operands.append(total)
    specs += [
        block_a,
        pl.BlockSpec(
            (depth, half), lambda i, place: (chunk, split * place[1] + lax.bitwise_xor(place[0], i))
        ),
    ]
    operands += [attended, w_out]
    for other, (near, far) in zip(other_attended, other_weights):
        specs += [block_a, block_w, block_w]
        operands += [other, near, far]
    if back is not None:
        specs.append(pl.BlockSpec(back.shape, lambda i, place: (0, 0)))
        operands.append(back)
    last = back is not None
    count = 1 + len(other_attended)
    return pl.pallas_call(
        functools.partial(
            finish_body, others=len(other_attended), has_sum=total is not None, last=last
        ),
        grid_spec=pltpu.PrefetchScalarGridSpec(
            num_scalar_prefetch=1,
            grid=(split,),
            in_specs=specs,
            out_specs=pl.BlockSpec((rows, half), mine),
        ),
        out_shape=jax.ShapeDtypeStruct((rows, out_width), bf16 if last else f32),
        compiler_params=pltpu.CompilerParams(vmem_limit_bytes=40 * mib),
        cost_estimate=cost(
            2 * rows * depth * count * out_width, 2 * depth * count * out_width + 8 * rows * out_width
        ),
        name="finish",
    )(place, *operands)


def flip(values, axis, mask):
    size = lax.axis_size(axis)
    return lax.ppermute(values, axis, [(i, i ^ mask) for i in range(size)])


def gather_counts(count):
    shards = lax.axis_size("seq")
    found = count.reshape(1)
    mask = 1
    while mask < shards:
        found = jnp.concatenate([found, flip(found, "seq", mask)])
        mask *= 2
    return found


def per_device(tokens, survive, norm_gain, w_qkv, qk_gain, w_out):
    positions = tokens.shape[0]
    heads, size = qk_gain.shape[1], qk_gain.shape[2]
    shards, head_shards = lax.axis_size("seq"), lax.axis_size("head")
    out_width = w_out.shape[1] // head_shards
    split = column_split(out_width)
    half = out_width // split
    groups = math.gcd(heads & -heads, shards)
    ring = shards // groups
    chunks = heads // groups
    me, side = lax.axis_index("seq"), lax.axis_index("head")
    core = me % split
    teams = [[r + ring * g for g in range(groups)] for r in range(ring)]

    def swap(values):
        if groups == 1:
            return values
        return lax.all_to_all(
            values, "seq", split_axis=0, concat_axis=0, axis_index_groups=teams, tiled=True
        )

    counts_by_mask = gather_counts(jnp.sum(survive))
    plane = me // ring
    masks = list(range(ring))
    wanted = jnp.array(
        [mask for mask in masks for _ in range(groups)] + [0] * groups, jnp.int32
    ) + ring * lax.bitwise_xor(
        jnp.array(list(range(groups)) * (ring + 1), jnp.int32), plane.astype(jnp.int32)
    )
    counts = counts_by_mask[wanted]

    normed, back = pack(tokens, survive, norm_gain)
    weights = jnp.transpose(w_qkv, (1, 0, 2))

    other_weights = []
    for mask in range(1, head_shards):
        column = lax.bitwise_xor(side, mask) * out_width + core * half
        near = flip(
            lax.dynamic_slice(w_out, (0, column), (w_out.shape[0], half)), "head", mask
        )
        other_weights.append((near, flip(near, "seq", 1) if split == 2 else near))

    place = jnp.stack([core, side]).astype(jnp.int32)
    total = None
    for chunk in range(chunks):
        keyval, query = project(normed, weights, qk_gain, chunk, groups)
        keyval = swap(keyval)
        query = swap(query)
        blocks = {0: keyval}
        mask = ring // 2
        while mask:
            for found in list(blocks):
                blocks[found | mask] = flip(blocks[found], "seq", mask)
            mask //= 2
        attended = attend(counts, query, [blocks[mask] for mask in masks], shards)
        attended = swap(attended)
        others = [flip(attended, "head", mask) for mask in range(1, head_shards)]
        total = finish(
            place,
            total,
            attended,
            w_out,
            others,
            other_weights,
            back if chunk == chunks - 1 else None,
            chunk,
            out_width,
        )
    return total


def solution(mesh):
    placed = (
        P("seq", None),
        P("seq"),
        P(),
        P(None, None, "head"),
        P(None, "head", None),
        P("head", None),
    )
    return jax.shard_map(
        per_device, mesh=mesh, in_specs=placed, out_specs=P("seq", "head"), check_vma=False
    )
```

time: 437 us -> 222 us (0.51)
  the two profiles are of different devices: /device:TPU:0 before, /device:TPU:1 now
where the time goes in v1:
time: 222 us; the launch traced here: 219 us
  Pallas kernels  70.3 us (32%)
  waiting for transfers between devices  66.8 us (30%)
  starting transfers between devices  59.5 us (27%)
  local copies, waits for them, and re-layouts  16.7 us (8%)
  other arithmetic  5.4 us (2%)
    all_to_all x9, waiting for transfers between devices, swap(): lax.all_to_all(values, 'seq', split_axis=0, concat_axis=0, axis_index_gro...  50.5 us
    all_to_all x9, starting transfers between devices, swap(): lax.all_to_all(values, 'seq', split_axis=0, concat_axis=0, axis_index_gro...  38.8 us
    pallas_call x3, Pallas kernels, project(): pl.pallas_call(functools.partial(project_body, first_head=chunk * groups,...  28.9 us
    pallas_call x3, Pallas kernels, attend(): pl.pallas_call(functools.partial(attend_body, sources=sources, key_room=k...  24.6 us
    ppermute x18, starting transfers between devices, flip(): return lax.ppermute(values, axis, [(i, i ^ mask) for i in range(size)])  20.7 us
    ppermute x18, waiting for transfers between devices, flip(): return lax.ppermute(values, axis, [(i, i ^ mask) for i in range(size)])  16.3 us
    pallas_call x3, Pallas kernels, finish(): pl.pallas_call(functools.partial(finish_body, others=len(other_attended),...  13 us
    unnamed x29, local copies, waits for them, and re-layouts  9.32 us
  transfers between devices with their start and end apart: 27, of which 11 were waited for; matrix products, arithmetic and copies ran while one was open for 5% of the time, Pallas kernels for 24%

profile of v1, /device:TPU:1, one launch (start us, length us, event | category | flops | bytes accessed | tf_op | source)
XLA Modules:
  0.0 218.9 jit_solution(1156348003188269267)
XLA Ops:
  2.2 1.7 copy-done.9
  4.6 3.8 %pack.1 = (bf16[384,3072]{1,0:T(8,128)(2,1)S(1)}, bf16[384,384]{1,0:T(8,128)(2,1)S(1)}) custom-call(s32[1,384]{1,0:T(1,128)S(1)} %reshape.13.row_ref, s32[384,1]{1,0:T(8,128)S(1)} %reshape.25.col_ref, bf16[384,3072]{1,0:T(8,128)(2,1)S(1)} %copy-done.9, f32[1,3072]{1,0:T(1,128)S(1)} %bitcast.5), custom_call_target="tpu_custom_call" | custom-call | flops 905969664 | bytes 4718592 | tf_op jit(solution)/shard_map/pack/pallas_call | solution.py:56
  9.1 9.6 %project.5 = (bf16[4,384,256]{2,1,0:T(8,128)(2,1)S(1)}, bf16[4,384,128]{2,1,0:T(8,128)(2,1)}) custom-call(bf16[384,3072]{1,0:T(8,128)(2,1)S(1)} %get-tuple-element.13.normed_ref, bf16[3,3072,1536]{2,1,0:T(8,128)(2,1)} %bitcast.6, f32[2,12,128]{2,1,0:T(8,128)S(1)} %copy.13.gain_ref), custom_call_target="tpu_custom_call" | custom-call | flops 3623878656 | bytes 11796480 | tf_op jit(solution)/shard_map/project/pallas_call | solution.py:115
  19.5 5.4 %all-to-all-start.6 = ((bf16[4,384,128]{2,1,0:T(8,128)(2,1)}), bf16[4,384,128]{2,1,0:T(8,128)(2,1)S(1)}, u32[]{:S(2)}, u32[]{:S(2)}) async-start(bf16[4,384,128]{2,1,0:T(8,128)(2,1)} %get-tuple-element.18), calls=%async_computation.6 | async-start | bytes 786432 | tf_op jit(solution)/shard_map/all_to_all | solution.py:359
  24.9 9.8 %project.4 = (bf16[4,384,256]{2,1,0:T(8,128)(2,1)}, bf16[4,384,128]{2,1,0:T(8,128)(2,1)}) custom-call(bf16[384,3072]{1,0:T(8,128)(2,1)S(1)} %get-tuple-element.13.normed_ref, bf16[3,3072,1536]{2,1,0:T(8,128)(2,1)} %bitcast.7, f32[2,12,128]{2,1,0:T(8,128)S(1)} %copy.13.gain_ref), custom_call_target="tpu_custom_call" | custom-call | flops 3623878656 | bytes 11796480 | tf_op jit(solution)/shard_map/project/pallas_call | solution.py:115
  34.7 1.1 all-to-all-done.6.query_ref
  35.8 4.2 %all-to-all-start.4 = ((bf16[4,384,256]{2,1,0:T(8,128)(2,1)}), bf16[4,384,256]{2,1,0:T(8,128)(2,1)}, u32[]{:S(2)}, u32[]{:S(2)}) async-start(bf16[4,384,256]{2,1,0:T(8,128)(2,1)} %get-tuple-element.17), calls=%async_computation.4 | async-start | bytes 1572864 | tf_op jit(solution)/shard_map/all_to_all | solution.py:359
  40.0 9.6 %project.3 = (bf16[4,384,256]{2,1,0:T(8,128)(2,1)S(1)}, bf16[4,384,128]{2,1,0:T(8,128)(2,1)}) custom-call(bf16[384,3072]{1,0:T(8,128)(2,1)S(1)} %get-tuple-element.13.normed_ref, bf16[3,3072,1536]{2,1,0:T(8,128)(2,1)} %bitcast.8, f32[2,12,128]{2,1,0:T(8,128)S(1)} %copy.13.gain_ref), custom_call_target="tpu_custom_call" | custom-call | flops 3623878656 | bytes 11796480 | tf_op jit(solution)/shard_map/project/pallas_call | solution.py:115
  50.5 9.2 %all-to-all-done.4.refs_0_ = bf16[4,384,256]{2,1,0:T(8,128)(2,1)} async-done(((bf16[4,384,256]{2,1,0:T(8,128)(2,1)}), bf16[4,384,256]{2,1,0:T(8,128)(2,1)}, u32[]{:S(2)}, u32[]{:S(2)}) %all-to-all-start.4) | async-done | bytes 786464 | tf_op jit(solution)/shard_map/all_to_all | solution.py:359
  59.7 3.5 %all-to-all-start.1 = ((bf16[4,384,256]{2,1,0:T(8,128)(2,1)}), bf16[4,384,256]{2,1,0:T(8,128)(2,1)S(1)}, u32[]{:S(2)}, u32[]{:S(2)}) async-start(bf16[4,384,256]{2,1,0:T(8,128)(2,1)} %copy-done.1), calls=%async_computation.1 | async-start | bytes 1572864 | tf_op jit(solution)/shard_map/all_to_all | solution.py:359
  63.2 3.2 %constant_dynamic-slice_fusion = bf16[1536,768]{1,0:T(8,128)(2,1)} fusion(bf16[1536,3072]{1,0:T(8,128)(2,1)} %refs_2_.3, s32[]{:T(128)S(6)} %select_n.20), kind=kLoop, calls=%fused_computation.7 | loop fusion | bytes 4718596 | tf_op jit(solution)/shard_map/dynamic_slice | solution.py:380
  66.5 1.2 collective-permute-start.8
  67.6 15.1 %all-to-all-done.1.refs_0_ = bf16[4,384,256]{2,1,0:T(8,128)(2,1)S(1)} async-done(((bf16[4,384,256]{2,1,0:T(8,128)(2,1)}), bf16[4,384,256]{2,1,0:T(8,128)(2,1)S(1)}, u32[]{:S(2)}, u32[]{:S(2)}) %all-to-all-start.1) | async-done | bytes 786464 | tf_op jit(solution)/shard_map/all_to_all | solution.py:359
  82.8 4.2 %all-to-all-start.7 = ((bf16[4,384,256]{2,1,0:T(8,128)(2,1)}), bf16[4,384,256]{2,1,0:T(8,128)(2,1)}, u32[]{:S(2)}, u32[]{:S(2)}) async-start(bf16[4,384,256]{2,1,0:T(8,128)(2,1)} %copy-done), calls=%async_computation.7 | async-start | bytes 1572864 | tf_op jit(solution)/shard_map/all_to_all | solution.py:359
  87.0 1.3 collective-permute-start.11
  88.2 1.7 collective-permute-start.10
  90.2 16.4 %all-to-all-done.7.refs_0_ = bf16[4,384,256]{2,1,0:T(8,128)(2,1)} async-done(((bf16[4,384,256]{2,1,0:T(8,128)(2,1)}), bf16[4,384,256]{2,1,0:T(8,128)(2,1)}, u32[]{:S(2)}, u32[]{:S(2)}) %all-to-all-start.7) | async-done | bytes 786464 | tf_op jit(solution)/shard_map/all_to_all | solution.py:359
  106.6 3.5 %all-to-all-start.3 = ((bf16[4,384,128]{2,1,0:T(8,128)(2,1)}), bf16[4,384,128]{2,1,0:T(8,128)(2,1)S(1)}, u32[]{:S(2)}, u32[]{:S(2)}) async-start(bf16[4,384,128]{2,1,0:T(8,128)(2,1)} %get-tuple-element.16), calls=%async_computation.3 | async-start | bytes 786432 | tf_op jit(solution)/shard_map/all_to_all | solution.py:359
  110.1 1.5 collective-permute-start.12
  112.3 1.6 collective-permute-done
  113.9 1.3 pad_add_fusion.1
  115.2 1.2 collective-permute-start.1
  116.4 5.3 %collective-permute-done.1 = s32[2]{0:T(128)S(1)} collective-permute-done((s32[2]{0:T(128)S(1)}, s32[2]{0:T(128)S(1)}, u32[]{:S(2)}, u32[]{:S(2)}) %collective-permute-start.1) | collective-permute-done | bytes 40 | tf_op jit(solution)/shard_map/ppermute | solution.py:329
  121.8 1.3 pad_add_fusion.2
  123.1 1.1 collective-permute-start.2
  124.2 1.3 collective-permute-done.2
  125.5 1.3 pad_add_fusion.3
  126.8 2.0 collective-permute-start.3
  128.8 1.3 collective-permute-done.3
  130.7 1.2 collective-permute-start.15
  131.9 4.1 %all-to-all-start = ((bf16[4,384,128]{2,1,0:T(8,128)(2,1)}), bf16[4,384,128]{2,1,0:T(8,128)(2,1)}, u32[]{:S(2)}, u32[]{:S(2)}) async-start(bf16[4,384,128]{2,1,0:T(8,128)(2,1)} %get-tuple-element.14), calls=%async_computation | async-start | bytes 786432 | tf_op jit(solution)/shard_map/all_to_all | solution.py:359
  136.1 5.5 %collective-permute-start.4 = (bf16[4,384,256]{2,1,0:T(8,128)(2,1)S(1)}, bf16[4,384,256]{2,1,0:T(8,128)(2,1)}, u32[]{:S(2)}, u32[]{:S(2)}) collective-permute-start(bf16[4,384,256]{2,1,0:T(8,128)(2,1)S(1)} %all-to-all-done.1.refs_0_), channel_id=1, source_target_pairs={{0,2},{2,0},{4,6},{6,4},{8,10},{10,8},{12,14},{14,12},{16,18},{18,... | collective-permute-start | bytes 2359304 | tf_op jit(solution)/shard_map/ppermute | solution.py:329
  142.8 2.0 concatenate.18
  145.4 8.2 %attend.4 = bf16[4,384,128]{2,1,0:T(8,128)(2,1)S(1)} custom-call(s32[20]{0:T(128)S(1)} %gather_fusion, bf16[4,384,128]{2,1,0:T(8,128)(2,1)S(1)} %all-to-all-done.3.query_ref, bf16[4,384,256]{2,1,0:T(8,128)(2,1)} %all-to-all-done.4.refs_0_, bf16[4,384,256]{2,1,0:T(8,128)(2,1)} %collective-permute-done.10.refs_1_, ...), custom_call_target="tpu_custom_call" | custom-call | flops 2415919104 | bytes 3145728 | tf_op jit(solution)/shard_map/attend/pallas_call | solution.py:226
  154.4 4.8 %all-to-all-start.5 = ((bf16[4,384,128]{2,1,0:T(8,128)(2,1)}), bf16[4,384,128]{2,1,0:T(8,128)(2,1)S(1)}, u32[]{:S(2)}, u32[]{:S(2)}) async-start(bf16[4,384,128]{2,1,0:T(8,128)(2,1)} %copy-done.4), calls=%async_computation.5 | async-start | bytes 786432 | tf_op jit(solution)/shard_map/all_to_all | solution.py:359
  159.7 8.2 %attend.3 = bf16[4,384,128]{2,1,0:T(8,128)(2,1)S(1)} custom-call(s32[20]{0:T(128)S(1)} %gather_fusion, bf16[4,384,128]{2,1,0:T(8,128)(2,1)} %all-to-all-done.query_ref, bf16[4,384,256]{2,1,0:T(8,128)(2,1)S(1)} %all-to-all-done.1.refs_0_, bf16[4,384,256]{2,1,0:T(8,128)(2,1)} %collective-permute-done.4.refs_1_, ...), custom_call_target="tpu_custom_call" | custom-call | flops 2415919104 | bytes 3145728 | tf_op jit(solution)/shard_map/attend/pallas_call | solution.py:226
  168.7 4.5 %all-to-all-start.2 = ((bf16[4,384,128]{2,1,0:T(8,128)(2,1)}), bf16[4,384,128]{2,1,0:T(8,128)(2,1)S(1)}, u32[]{:S(2)}, u32[]{:S(2)}) async-start(bf16[4,384,128]{2,1,0:T(8,128)(2,1)} %copy-done.5), calls=%async_computation.2 | async-start | bytes 786432 | tf_op jit(solution)/shard_map/all_to_all | solution.py:359
  173.3 1.0 copy-done.3
  174.3 8.2 %attend.5 = bf16[4,384,128]{2,1,0:T(8,128)(2,1)S(1)} custom-call(s32[20]{0:T(128)S(1)} %gather_fusion, bf16[4,384,128]{2,1,0:T(8,128)(2,1)S(1)} %copy-done.3, bf16[4,384,256]{2,1,0:T(8,128)(2,1)} %all-to-all-done.7.refs_0_, bf16[4,384,256]{2,1,0:T(8,128)(2,1)} %collective-permute-done.14.refs_1_, bf16[4,384,256]{2,1,0:T(8,128)(2,1)} %collective-permute-done.15.refs_2_, ...), custom_call_target="tpu_custom_call" | custom-call | flops 2415919104 | bytes 3145728 | tf_op jit(solution)/shard_map/attend/pallas_call | solution.py:226
  183.2 4.5 %all-to-all-start.8 = ((bf16[4,384,128]{2,1,0:T(8,128)(2,1)}), bf16[4,384,128]{2,1,0:T(8,128)(2,1)S(1)}, u32[]{:S(2)}, u32[]{:S(2)}) async-start(bf16[4,384,128]{2,1,0:T(8,128)(2,1)} %copy-done.6), calls=%async_computation.8 | async-start | bytes 786432 | tf_op jit(solution)/shard_map/all_to_all | solution.py:359
  187.8 1.2 collective-permute-start.7
  189.2 8.7 %all-to-all-done.8.refs_1_ = bf16[4,384,128]{2,1,0:T(8,128)(2,1)S(1)} async-done(((bf16[4,384,128]{2,1,0:T(8,128)(2,1)}), bf16[4,384,128]{2,1,0:T(8,128)(2,1)S(1)}, u32[]{:S(2)}, u32[]{:S(2)}) %all-to-all-start.8) | async-done | bytes 393248 | tf_op jit(solution)/shard_map/all_to_all | solution.py:359
  197.9 1.2 collective-permute-start.17
  199.2 3.8 %finish.3.refs_0_ = f32[384,1536]{1,0:T(8,128)S(1)} custom-call(s32[2]{0:T(128)S(1)} %pad_add_fusion.place_ref, bf16[4,384,128]{2,1,0:T(8,128)(2,1)S(1)} %all-to-all-done.2.refs_0_, bf16[1536,3072]{1,0:T(8,128)(2,1)} %refs_2_.3, bf16[4,384,128]{2,1,0:T(8,128)(2,1)} %collective-permute-done.7.refs_2_, ...), custom_call_target="tpu_custom_call" | custom-call | flops 1207959552 | bytes 7864320 | tf_op jit(solution)/shard_map/finish/pallas_call | solution.py:308
  203.0 4.4 %collective-permute-done.13.refs_3_ = bf16[4,384,128]{2,1,0:T(8,128)(2,1)} collective-permute-done((bf16[4,384,128]{2,1,0:T(8,128)(2,1)S(1)}, bf16[4,384,128]{2,1,0:T(8,128)(2,1)}, u32[]{:S(2)}, u32[]{:S(2)}) %collective-permute-start.13) | collective-permute-done | bytes 393248 | tf_op jit(solution)/shard_map/ppermute | solution.py:329
  207.4 3.9 %finish.4.refs_0_ = f32[384,1536]{1,0:T(8,128)S(1)} custom-call(s32[2]{0:T(128)S(1)} %pad_add_fusion.place_ref, f32[384,1536]{1,0:T(8,128)S(1)} %finish.3.refs_0_, bf16[4,384,128]{2,1,0:T(8,128)(2,1)S(1)} %all-to-all-done.5.refs_1_, bf16[1536,3072]{1,0:T(8,128)(2,1)} %refs_2_.3, bf16[4,384,128]{2,1,0:T(8,128)(2,1)} %collective-permute-done.13.refs_3_, ...), custom_call_target="tpu_custom_call" | custom-call | flops 1207959552 | bytes 7864320 | tf_op jit(solution)/shard_map/finish/pallas_call | solution.py:308
  211.3 2.4 %collective-permute-done.17.refs_3_ = bf16[4,384,128]{2,1,0:T(8,128)(2,1)S(1)} collective-permute-done((bf16[4,384,128]{2,1,0:T(8,128)(2,1)S(1)}, bf16[4,384,128]{2,1,0:T(8,128)(2,1)S(1)}, u32[]{:S(2)}, u32[]{:S(2)}) %collective-permute-start.17) | collective-permute-done | bytes 393248 | tf_op jit(solution)/shard_map/ppermute | solution.py:329
  213.7 5.3 %finish.5 = bf16[384,1536]{1,0:T(8,128)(2,1)} custom-call(s32[2]{0:T(128)S(1)} %pad_add_fusion.place_ref, f32[384,1536]{1,0:T(8,128)S(1)} %finish.4.refs_0_, bf16[4,384,128]{2,1,0:T(8,128)(2,1)S(1)} %all-to-all-done.8.refs_1_, bf16[1536,3072]{1,0:T(8,128)(2,1)} %refs_2_.3, bf16[4,384,128]{2,1,0:T(8,128)(2,1)S(1)} %collective-permute-done.17.refs_3_, ...), custom_call_target="tpu_custom_call" | custom-call | flops 1207959552 | bytes 7864320 | tf_op jit(solution)/shard_map/finish/pallas_call | solution.py:308
  (57 shorter events, 11.8 us)
Async XLA Ops:
  2.2 1.7 copy-start.9
  3.9 0.7 copy-start.10
  8.4 0.7 copy-start.7
  18.6 0.9 copy-start
  19.5 16.3 %all-to-all-start.6 = ((bf16[4,384,128]{2,1,0:T(8,128)(2,1)}), bf16[4,384,128]{2,1,0:T(8,128)(2,1)S(1)}, u32[]{:S(2)}, u32[]{:S(2)}) async-start(bf16[4,384,128]{2,1,0:T(8,128)(2,1)} %get-tuple-element.18), calls=%async_computation.6 | async-start | bytes 786432 | tf_op jit(solution)/shard_map/all_to_all | solution.py:359
  35.8 13.8 %copy-start.2 = (bf16[4,384,128]{2,1,0:T(8,128)(2,1)}, bf16[4,384,128]{2,1,0:T(8,128)(2,1)S(1)}, u32[]{:S(2)}) copy-start(bf16[4,384,128]{2,1,0:T(8,128)(2,1)S(1)} %all-to-all-done.6.query_ref) | copy-start | bytes 1179652
  35.8 23.9 %all-to-all-start.4 = ((bf16[4,384,256]{2,1,0:T(8,128)(2,1)}), bf16[4,384,256]{2,1,0:T(8,128)(2,1)}, u32[]{:S(2)}, u32[]{:S(2)}) async-start(bf16[4,384,256]{2,1,0:T(8,128)(2,1)} %get-tuple-element.17), calls=%async_computation.4 | async-start | bytes 1572864 | tf_op jit(solution)/shard_map/all_to_all | solution.py:359
  49.6 0.9 copy-start.1
  59.7 23.1 %all-to-all-start.1 = ((bf16[4,384,256]{2,1,0:T(8,128)(2,1)}), bf16[4,384,256]{2,1,0:T(8,128)(2,1)S(1)}, u32[]{:S(2)}, u32[]{:S(2)}) async-start(bf16[4,384,256]{2,1,0:T(8,128)(2,1)} %copy-done.1), calls=%async_computation.1 | async-start | bytes 1572864 | tf_op jit(solution)/shard_map/all_to_all | solution.py:359
  66.4 45.2 %copy-start.11 = (s32[384]{0:T(512)S(1)}, s32[384]{0:T(512)}, u32[]{:S(2)}) copy-start(s32[384]{0:T(512)} %param.9) | copy-start | bytes 4612
  66.5 75.7 %copy-start.12 = (s32[20]{0:T(128)S(1)}, s32[20]{0:T(128)}, u32[]{:S(2)}) copy-start(s32[20]{0:T(128)} %constant.51.clone) | copy-start | bytes 244
  66.5 75.2 %collective-permute-start.8 = (bf16[1536,768]{1,0:T(8,128)(2,1)}, bf16[1536,768]{1,0:T(8,128)(2,1)S(1)}, u32[]{:S(2)}, u32[]{:S(2)}) collective-permute-start(bf16[1536,768]{1,0:T(8,128)(2,1)} %constant_dynamic-slice_fusion), channel_id=1, source_target_pairs={{0,1},{1,0},{2,3},{3,2},{4,5},{5,4},{6,7},{7,6},{8,9},{9,8},{10,11... | collective-permute-start | bytes 7077896 | tf_op jit(solution)/shard_map/ppermute | solution.py:329
  82.8 23.9 %all-to-all-start.7 = ((bf16[4,384,256]{2,1,0:T(8,128)(2,1)}), bf16[4,384,256]{2,1,0:T(8,128)(2,1)}, u32[]{:S(2)}, u32[]{:S(2)}) async-start(bf16[4,384,256]{2,1,0:T(8,128)(2,1)} %copy-done), calls=%async_computation.7 | async-start | bytes 1572864 | tf_op jit(solution)/shard_map/all_to_all | solution.py:359
  87.0 23.1 %collective-permute-start.11 = (bf16[4,384,256]{2,1,0:T(8,128)(2,1)}, bf16[4,384,256]{2,1,0:T(8,128)(2,1)}, u32[]{:S(2)}, u32[]{:S(2)}) collective-permute-start(bf16[4,384,256]{2,1,0:T(8,128)(2,1)} %all-to-all-done.4.refs_0_), channel_id=1, source_target_pairs={{0,4},{2,6},{4,0},{6,2},{8,12},{10,14},{12,8},{14,10},{16,20},{18,... | collective-permute-start | bytes 2359304 | tf_op jit(solution)/shard_map/ppermute | solution.py:329
  88.2 47.8 %collective-permute-start.10 = (bf16[4,384,256]{2,1,0:T(8,128)(2,1)}, bf16[4,384,256]{2,1,0:T(8,128)(2,1)}, u32[]{:S(2)}, u32[]{:S(2)}) collective-permute-start(bf16[4,384,256]{2,1,0:T(8,128)(2,1)} %all-to-all-done.4.refs_0_), channel_id=1, source_target_pairs={{0,2},{2,0},{4,6},{6,4},{8,10},{10,8},{12,14},{14,12},{16,18},{18,... | collective-permute-start | bytes 2359304 | tf_op jit(solution)/shard_map/ppermute | solution.py:329
  90.0 51.6 %collective-permute-start.5 = (bf16[4,384,256]{2,1,0:T(8,128)(2,1)S(1)}, bf16[4,384,256]{2,1,0:T(8,128)(2,1)}, u32[]{:S(2)}, u32[]{:S(2)}) collective-permute-start(bf16[4,384,256]{2,1,0:T(8,128)(2,1)S(1)} %all-to-all-done.1.refs_0_), channel_id=1, source_target_pairs={{0,4},{2,6},{4,0},{6,2},{8,12},{10,14},{12,8},{14,10},{16,20},{18,... | collective-permute-start | bytes 2359304 | tf_op jit(solution)/shard_map/ppermute | solution.py:329
  106.6 25.3 %all-to-all-start.3 = ((bf16[4,384,128]{2,1,0:T(8,128)(2,1)}), bf16[4,384,128]{2,1,0:T(8,128)(2,1)S(1)}, u32[]{:S(2)}, u32[]{:S(2)}) async-start(bf16[4,384,128]{2,1,0:T(8,128)(2,1)} %get-tuple-element.16), calls=%async_computation.3 | async-start | bytes 786432 | tf_op jit(solution)/shard_map/all_to_all | solution.py:359
  110.1 35.3 %collective-permute-start.12 = (bf16[4,384,256]{2,1,0:T(8,128)(2,1)}, bf16[4,384,256]{2,1,0:T(8,128)(2,1)}, u32[]{:S(2)}, u32[]{:S(2)}) collective-permute-start(bf16[4,384,256]{2,1,0:T(8,128)(2,1)} %collective-permute-done.11.refs_2_), channel_id=1, source_target_pairs={{0,2},{2,0},{4,6},{6,4},{8,10},{10,8},{12,14},{14,12},{16,18},{18,... | collective-permute-start | bytes 2359304 | tf_op jit(solution)/shard_map/ppermute | solution.py:329
  112.3 1.6 collective-permute-start
  115.2 6.5 %collective-permute-start.1 = (s32[2]{0:T(128)S(1)}, s32[2]{0:T(128)S(1)}, u32[]{:S(2)}, u32[]{:S(2)}) collective-permute-start(s32[2]{0:T(128)S(1)} %pad_add_fusion.1), channel_id=1, source_target_pairs={{0,4},{2,6},{4,0},{6,2},{8,12},{10,14},{12,8},{14,10},{16,20},{18,... | collective-permute-start | bytes 32 | tf_op jit(solution)/shard_map/ppermute | solution.py:329
  123.1 2.4 %collective-permute-start.2 = (s32[4]{0:T(128)S(1)}, s32[4]{0:T(128)S(1)}, u32[]{:S(2)}, u32[]{:S(2)}) collective-permute-start(s32[4]{0:T(128)S(1)} %pad_add_fusion.2), channel_id=1, source_target_pairs={{0,8},{2,10},{4,12},{6,14},{8,0},{10,2},{12,4},{14,6},{16,24},{18,... | collective-permute-start | bytes 56 | tf_op jit(solution)/shard_map/ppermute | solution.py:329
  126.8 3.3 %collective-permute-start.3 = (s32[8]{0:T(128)S(1)}, s32[8]{0:T(128)S(1)}, u32[]{:S(2)}, u32[]{:S(2)}) collective-permute-start(s32[8]{0:T(128)S(1)} %pad_add_fusion.3), channel_id=1, source_target_pairs={{0,16},{2,18},{4,20},{6,22},{8,24},{10,26},{12,28},{14,30},{16,0},... | collective-permute-start | bytes 104 | tf_op jit(solution)/shard_map/ppermute | solution.py:329
  130.1 0.5 copy-start.13
  130.7 28.5 %collective-permute-start.15 = (bf16[4,384,256]{2,1,0:T(8,128)(2,1)}, bf16[4,384,256]{2,1,0:T(8,128)(2,1)}, u32[]{:S(2)}, u32[]{:S(2)}) collective-permute-start(bf16[4,384,256]{2,1,0:T(8,128)(2,1)} %all-to-all-done.7.refs_0_), channel_id=1, source_target_pairs={{0,4},{2,6},{4,0},{6,2},{8,12},{10,14},{12,8},{14,10},{16,20},{18,... | collective-permute-start | bytes 2359304 | tf_op jit(solution)/shard_map/ppermute | solution.py:329
  131.9 22.5 %all-to-all-start = ((bf16[4,384,128]{2,1,0:T(8,128)(2,1)}), bf16[4,384,128]{2,1,0:T(8,128)(2,1)}, u32[]{:S(2)}, u32[]{:S(2)}) async-start(bf16[4,384,128]{2,1,0:T(8,128)(2,1)} %get-tuple-element.14), calls=%async_computation | async-start | bytes 786432 | tf_op jit(solution)/shard_map/all_to_all | solution.py:359
  136.1 23.7 %collective-permute-start.4 = (bf16[4,384,256]{2,1,0:T(8,128)(2,1)S(1)}, bf16[4,384,256]{2,1,0:T(8,128)(2,1)}, u32[]{:S(2)}, u32[]{:S(2)}) collective-permute-start(bf16[4,384,256]{2,1,0:T(8,128)(2,1)S(1)} %all-to-all-done.1.refs_0_), channel_id=1, source_target_pairs={{0,2},{2,0},{4,6},{6,4},{8,10},{10,8},{12,14},{14,12},{16,18},{18,... | collective-permute-start | bytes 2359304 | tf_op jit(solution)/shard_map/ppermute | solution.py:329
  141.6 18.1 %collective-permute-start.6 = (bf16[4,384,256]{2,1,0:T(8,128)(2,1)}, bf16[4,384,256]{2,1,0:T(8,128)(2,1)}, u32[]{:S(2)}, u32[]{:S(2)}) collective-permute-start(bf16[4,384,256]{2,1,0:T(8,128)(2,1)} %collective-permute-done.5.refs_2_), channel_id=1, source_target_pairs={{0,2},{2,0},{4,6},{6,4},{8,10},{10,8},{12,14},{14,12},{16,18},{18,... | collective-permute-start | bytes 2359304 | tf_op jit(solution)/shard_map/ppermute | solution.py:329
  141.7 57.5 %collective-permute-start.9 = (bf16[1536,768]{1,0:T(8,128)(2,1)S(1)}, bf16[1536,768]{1,0:T(8,128)(2,1)}, u32[]{:S(2)}, u32[]{:S(2)}) collective-permute-start(bf16[1536,768]{1,0:T(8,128)(2,1)S(1)} %collective-permute-done.8.refs_3_.refs_4_), channel_id=1, source_target_pairs={{0,2},{2,0},{4,6},{6,4},{8,10},{10,8},{12,14},{14,12},{16,18},{18,... | collective-permute-start | bytes 7077896 | tf_op jit(solution)/shard_map/ppermute | solution.py:329
  153.6 0.8 copy-start.4
  154.4 14.3 %all-to-all-start.5 = ((bf16[4,384,128]{2,1,0:T(8,128)(2,1)}), bf16[4,384,128]{2,1,0:T(8,128)(2,1)S(1)}, u32[]{:S(2)}, u32[]{:S(2)}) async-start(bf16[4,384,128]{2,1,0:T(8,128)(2,1)} %copy-done.4), calls=%async_computation.5 | async-start | bytes 786432 | tf_op jit(solution)/shard_map/all_to_all | solution.py:359
  159.2 14.1 %collective-permute-start.14 = (bf16[4,384,256]{2,1,0:T(8,128)(2,1)}, bf16[4,384,256]{2,1,0:T(8,128)(2,1)}, u32[]{:S(2)}, u32[]{:S(2)}) collective-permute-start(bf16[4,384,256]{2,1,0:T(8,128)(2,1)} %all-to-all-done.7.refs_0_), channel_id=1, source_target_pairs={{0,2},{2,0},{4,6},{6,4},{8,10},{10,8},{12,14},{14,12},{16,18},{18,... | collective-permute-start | bytes 2359304 | tf_op jit(solution)/shard_map/ppermute | solution.py:329
  159.2 14.1 %collective-permute-start.16 = (bf16[4,384,256]{2,1,0:T(8,128)(2,1)}, bf16[4,384,256]{2,1,0:T(8,128)(2,1)}, u32[]{:S(2)}, u32[]{:S(2)}) collective-permute-start(bf16[4,384,256]{2,1,0:T(8,128)(2,1)} %collective-permute-done.15.refs_2_), channel_id=1, source_target_pairs={{0,2},{2,0},{4,6},{6,4},{8,10},{10,8},{12,14},{14,12},{16,18},{18,... | collective-permute-start | bytes 2359304 | tf_op jit(solution)/shard_map/ppermute | solution.py:329
  168.0 0.7 copy-start.5
  168.7 14.5 %all-to-all-start.2 = ((bf16[4,384,128]{2,1,0:T(8,128)(2,1)}), bf16[4,384,128]{2,1,0:T(8,128)(2,1)S(1)}, u32[]{:S(2)}, u32[]{:S(2)}) async-start(bf16[4,384,128]{2,1,0:T(8,128)(2,1)} %copy-done.5), calls=%async_computation.2 | async-start | bytes 786432 | tf_op jit(solution)/shard_map/all_to_all | solution.py:359
  173.3 1.0 copy-start.3
  182.5 0.8 copy-start.6
  183.2 14.7 %all-to-all-start.8 = ((bf16[4,384,128]{2,1,0:T(8,128)(2,1)}), bf16[4,384,128]{2,1,0:T(8,128)(2,1)S(1)}, u32[]{:S(2)}, u32[]{:S(2)}) async-start(bf16[4,384,128]{2,1,0:T(8,128)(2,1)} %copy-done.6), calls=%async_computation.8 | async-start | bytes 786432 | tf_op jit(solution)/shard_map/all_to_all | solution.py:359
  187.8 11.4 %collective-permute-start.7 = (bf16[4,384,128]{2,1,0:T(8,128)(2,1)S(1)}, bf16[4,384,128]{2,1,0:T(8,128)(2,1)}, u32[]{:S(2)}, u32[]{:S(2)}) collective-permute-start(bf16[4,384,128]{2,1,0:T(8,128)(2,1)S(1)} %all-to-all-done.2.refs_0_), channel_id=1, source_target_pairs={{0,1},{1,0},{2,3},{3,2},{4,5},{5,4},{6,7},{7,6},{8,9},{9,8},{10,11... | collective-permute-start | bytes 1179656 | tf_op jit(solution)/shard_map/ppermute | solution.py:329
  189.0 18.4 %collective-permute-start.13 = (bf16[4,384,128]{2,1,0:T(8,128)(2,1)S(1)}, bf16[4,384,128]{2,1,0:T(8,128)(2,1)}, u32[]{:S(2)}, u32[]{:S(2)}) collective-permute-start(bf16[4,384,128]{2,1,0:T(8,128)(2,1)S(1)} %all-to-all-done.5.refs_1_), channel_id=1, source_target_pairs={{0,1},{1,0},{2,3},{3,2},{4,5},{5,4},{6,7},{7,6},{8,9},{9,8},{10,11... | collective-permute-start | bytes 1179656 | tf_op jit(solution)/shard_map/ppermute | solution.py:329
  197.9 15.7 %collective-permute-start.17 = (bf16[4,384,128]{2,1,0:T(8,128)(2,1)S(1)}, bf16[4,384,128]{2,1,0:T(8,128)(2,1)S(1)}, u32[]{:S(2)}, u32[]{:S(2)}) collective-permute-start(bf16[4,384,128]{2,1,0:T(8,128)(2,1)S(1)} %all-to-all-done.8.refs_1_), channel_id=1, source_target_pairs={{0,1},{1,0},{2,3},{3,2},{4,5},{5,4},{6,7},{7,6},{8,9},{9,8},{10,11... | collective-permute-start | bytes 1179656 | tf_op jit(solution)/shard_map/ppermute | solution.py:329
  203.0 10.7 %copy-start.8 = (bf16[384,384]{1,0:T(8,128)(2,1)S(1)}, bf16[384,384]{1,0:T(8,128)(2,1)}, u32[]{:S(2)}) copy-start(bf16[384,384]{1,0:T(8,128)(2,1)} %copy-done.7) | copy-start | bytes 884740

commit v2 on v1

v2 whole, which is shorter than its diff:
```python
import functools
import math

import jax
import jax.numpy as jnp
from jax import lax
from jax.experimental import pallas as pl
from jax.experimental.pallas import tpu as pltpu
from jax.sharding import PartitionSpec as P

epsilon = 1e-06
dead_mark = 1e30
dead_limit = 1e15
mib = 1 << 20
f32 = jnp.float32
bf16 = jnp.bfloat16
params = pltpu.CompilerParams(vmem_limit_bytes=60 * mib)


def cost(flops, bytes_accessed, exps=0):
    return pl.CostEstimate(
        flops=int(flops), bytes_accessed=int(bytes_accessed), transcendentals=int(exps)
    )


def flip(values, axis, mask):
    size = lax.axis_size(axis)
    return lax.ppermute(values, axis, [(i, i ^ mask) for i in range(size)])


def pack_body(survive_ref, tokens_ref, gain_ref, normed_ref, back_ref, count_ref, *, rows):
    positions = tokens_ref.shape[0]
    step = pl.program_id(0)
    first = lax.broadcasted_iota(jnp.int32, (positions, positions), 0)
    second = lax.broadcasted_iota(jnp.int32, (positions, positions), 1)
    live = jnp.broadcast_to(survive_ref[...].reshape(1, positions), (8, positions)).astype(f32)
    upper = (first <= second).astype(f32).astype(bf16)
    rank = jnp.dot(live.astype(bf16), upper, preferred_element_type=f32)
    target = jnp.where(live > 0.5, rank - 1.0, -1.0)
    slots = lax.broadcasted_iota(jnp.int32, (rows, positions), 0) + step * rows
    chosen = (slots == target[:1].astype(jnp.int32)).astype(f32).astype(bf16)
    packed = jnp.dot(chosen, tokens_ref[...], preferred_element_type=f32)
    center = packed - jnp.mean(packed, axis=-1, keepdims=True)
    spread = jnp.mean(center * center, axis=-1, keepdims=True)
    gain = gain_ref[...].reshape(1, gain_ref.shape[0])
    normed_ref[...] = (center * lax.rsqrt(spread + epsilon) * gain).astype(bf16)

    @pl.when(step == 0)
    def _():
        home = jnp.transpose(target)[:, :1].astype(jnp.int32)
        back_ref[...] = (second == home).astype(f32).astype(bf16)
        count_ref[0, 0] = jnp.max(rank).astype(jnp.int32)


def pack(tokens, survive, norm_gain):
    positions, width = tokens.shape
    rows = 128 if positions % 128 == 0 else positions
    return pl.pallas_call(
        functools.partial(pack_body, rows=rows),
        grid=(positions // rows,),
        in_specs=[
            pl.BlockSpec((positions,), lambda i: (0,)),
            pl.BlockSpec((positions, width), lambda i: (0, 0)),
            pl.BlockSpec((width,), lambda i: (0,)),
        ],
        out_specs=[
            pl.BlockSpec((rows, width), lambda i: (i, 0)),
            pl.BlockSpec((positions, positions), lambda i: (0, 0)),
            pl.BlockSpec(memory_space=pltpu.SMEM),
        ],
        out_shape=[
            jax.ShapeDtypeStruct((positions, width), bf16),
            jax.ShapeDtypeStruct((positions, positions), bf16),
            jax.ShapeDtypeStruct((1, 1), jnp.int32),
        ],
        compiler_params=params,
        cost_estimate=cost(2 * positions * positions * width, 4 * positions * width),
        name="pack",
    )(survive, tokens, norm_gain)


def project_body(place_ref, count_ref, normed_ref, weight_ref, gain_ref, *refs, kinds, chunks, groups, pair):
    outs, result_ref = list(refs[:-1]), refs[-1]
    keyval_refs = outs[:groups] if 1 in kinds else []
    query_refs = outs[-groups:] if 0 in kinds else []
    rows = normed_ref.shape[0]
    size = gain_ref.shape[2]
    wide = pair * size
    plane = place_ref[0]
    tile = lax.bitwise_xor(pl.program_id(1), plane // pair)
    head = (chunks[0] + pl.program_id(0)) * groups + tile * pair

    def write(refs, low, values, steps):
        result_ref[...] = values
        for n in range(groups // pair):

            @pl.when(pl.program_id(1) == n)
            def _():
                for i in range(pair):
                    start = pl.multiple_of(lax.bitwise_xor(plane % pair, i) * size, size)
                    found = result_ref[:, pl.ds(start, size)].astype(bf16)
                    refs[n * pair + i][0, :, low : low + size] = found

    for step, kind in enumerate(kinds):

        @pl.when(pl.program_id(2) == step)
        def _():
            result = jnp.dot(normed_ref[...], weight_ref[0], preferred_element_type=f32)
            if kind == 2:
                write(keyval_refs, size, result, step)
                return
            of_row = lax.broadcasted_iota(jnp.int32, (wide, wide), 0) // size
            of_col = lax.broadcasted_iota(jnp.int32, (wide, wide), 1) // size
            average = jnp.where(of_row == of_col, 1.0 / size, 0.0).astype(bf16)

            def mean(values):
                coarse = values.astype(bf16)
                fine = (values - coarse.astype(f32)).astype(bf16)
                return jnp.dot(coarse, average, preferred_element_type=f32) + jnp.dot(
                    fine, average, preferred_element_type=f32
                )

            center = result - mean(result)
            gain = jnp.concatenate(
                [gain_ref[head + i, kind : kind + 1, :] for i in range(pair)], axis=-1
            )
            if kind == 0:
                gain = gain * (1.0 / math.sqrt(size))
            normed = center * lax.rsqrt(mean(center * center) + epsilon) * gain
            if kind == 1:
                row = lax.broadcasted_iota(jnp.int32, (rows, wide), 0)
                normed = jnp.where(row < count_ref[0, 0], normed, dead_mark)
                write(keyval_refs, 0, normed, step)
            else:
                write(query_refs, 0, normed, step)


def project(place, count, normed, weights, gains, kinds, chunks, groups):
    rows, width = normed.shape
    size = gains.shape[2]
    pair = 2 if groups % 2 == 0 else 1
    tiles = groups // pair
    columns = pair * size

    def weight_index(c, n, t, place):
        kind = 0
        for step, value in enumerate(kinds):
            kind = jnp.where(t == step, value, kind)
        tile = lax.bitwise_xor(n, place[0] // pair)
        return (kind, 0, (chunks[0] + c) * tiles + tile)

    widths = ([2 * size] * groups if 1 in kinds else []) + ([size] * groups if 0 in kinds else [])
    found = pl.pallas_call(
        functools.partial(project_body, kinds=kinds, chunks=chunks, groups=groups, pair=pair),
        grid_spec=pltpu.PrefetchScalarGridSpec(
            num_scalar_prefetch=1,
            grid=(len(chunks), tiles, len(kinds)),
            in_specs=[
                pl.BlockSpec(memory_space=pltpu.SMEM),
                pl.BlockSpec((rows, width), lambda c, n, t, place: (0, 0)),
                pl.BlockSpec((1, width, columns), weight_index),
                pl.BlockSpec(gains.shape, lambda c, n, t, place: (0, 0, 0)),
            ],
            out_specs=[
                pl.BlockSpec((1, rows, wide), lambda c, n, t, place: (c, 0, 0)) for wide in widths
            ],
            scratch_shapes=[pltpu.VMEM((rows, columns), f32)],
        ),
        out_shape=[jax.ShapeDtypeStruct((len(chunks), rows, wide), bf16) for wide in widths],
        compiler_params=params,
        cost_estimate=cost(
            2 * rows * width * len(kinds) * len(chunks) * groups * size,
            2 * width * len(kinds) * len(chunks) * groups * size + 2 * rows * width,
        ),
        name="project",
    )(place, count, normed, weights, gains)
    keyval = found[:groups] if 1 in kinds else None
    query = found[-groups:] if 0 in kinds else None
    return keyval, query


def attend_body(*refs, groups, sources, key_room, query_rows, key_cols):
    query_refs = refs[:groups]
    keyval_refs = refs[groups : groups + sources]
    out_refs = refs[groups + sources : 2 * groups + sources]
    keys, values, queries, results = refs[2 * groups + sources :]
    rows, size = query_refs[0].shape[1:]
    piece = 128 if rows % 128 == 0 else rows
    align = lambda count: pl.multiple_of((count + 15) // 16 * 16, 16)
    line = lax.broadcasted_iota(jnp.int32, (piece, size), 0)

    counts = []
    for source in keyval_refs:
        for block in range(source.shape[0]):
            live = (source[block, :, :size].astype(f32) < dead_limit).astype(f32)
            counts.append(jnp.max(jnp.sum(live, axis=0, keepdims=True)).astype(jnp.int32))

    offset = jnp.int32(0)
    index = 0
    for source in keyval_refs:
        for block in range(source.shape[0]):
            count = counts[index]
            for part in range(rows // piece):

                @pl.when(part * piece < count)
                def _():
                    here = pl.ds(pl.multiple_of(offset + part * piece, 16), piece)
                    there = pl.ds(part * piece, piece)
                    live = line + part * piece < count
                    found = jnp.where(live, source[block, there, :size].astype(f32), 0.0)
                    keys[here, :] = found.astype(bf16)
                    values[here, :size] = source[block, there, size:]
                    values[here, size:] = live.astype(f32).astype(bf16)

            offset = pl.multiple_of(offset + align(count), 16)
            index += 1

    def clear(step, carry):
        here = pl.ds(pl.multiple_of(offset + step * 16, 16), 16)
        keys[here, :] = jnp.zeros((16, size), bf16)
        values[here, :] = jnp.zeros((16, 2 * size), bf16)
        return carry

    lax.fori_loop(0, (key_room - offset) // 16, clear, 0)

    starts = []
    start = jnp.int32(0)
    for block in range(groups):
        starts.append(start)
        for part in range(rows // piece):

            @pl.when(part * piece < counts[block])
            def _():
                here = pl.ds(pl.multiple_of(start + part * piece, 16), piece)
                queries[here, :] = query_refs[block][0, part * piece : (part + 1) * piece, :]

        start = pl.multiple_of(start + align(counts[block]), 16)

    def one_tile(tile, carry):
        here = pl.ds(pl.multiple_of(tile * query_rows, query_rows), query_rows)
        query = queries[here, :]
        total = jnp.zeros((query_rows, 2 * size), f32)
        for low in range(0, key_room, key_cols):
            high = min(low + key_cols, key_room)
            scores = lax.dot_general(
                query, keys[low:high, :], (((1,), (1,)), ((), ())), preferred_element_type=f32
            )
            weights = jnp.exp(scores).astype(bf16)
            total += jnp.dot(weights, values[low:high, :], preferred_element_type=f32)
        results[here, :] = (total[:, :size] / total[:, size:]).astype(bf16)
        return carry

    lax.fori_loop(0, (start + query_rows - 1) // query_rows, one_tile, 0)

    for block in range(groups):
        for part in range(rows // piece):
            here = pl.ds(pl.multiple_of(starts[block] + part * piece, 16), piece)
            live = line + part * piece < counts[block]
            out_refs[block][0, part * piece : (part + 1) * piece, :] = jnp.where(
                live, results[here, :].astype(f32), 0.0
            ).astype(bf16)


def attend(queries, which, keyvals, shards):
    groups = len(queries)
    rows, size = queries[0].shape[1:]
    running = shards * rows // 2
    key_room = -(-(running + 16 * shards) // 256) * 256
    query_rows = 256
    query_room = -(-groups * rows // query_rows) * query_rows + rows
    return pl.pallas_call(
        functools.partial(
            attend_body,
            groups=groups,
            sources=len(keyvals),
            key_room=key_room,
            query_rows=query_rows,
            key_cols=512,
        ),
        grid=(1,),
        in_specs=[pl.BlockSpec((1, rows, size), lambda i: (which, 0, 0))] * groups
        + [pl.BlockSpec(keyval.shape, lambda i: (0, 0, 0)) for keyval in keyvals],
        out_specs=[pl.BlockSpec((1, rows, size), lambda i: (0, 0, 0))] * groups,
        out_shape=[jax.ShapeDtypeStruct((1, rows, size), bf16)] * groups,
        scratch_shapes=[
            pltpu.VMEM((key_room + rows, size), bf16),
            pltpu.VMEM((key_room + rows, 2 * size), bf16),
            pltpu.VMEM((query_room, size), bf16),
            pltpu.VMEM((query_room, size), bf16),
        ],
        compiler_params=params,
        cost_estimate=cost(
            8 * groups * rows // 2 * running * size,
            4 * shards * rows * size,
            groups * rows // 2 * running,
        ),
        name="attend",
    )(*queries, *keyvals)


def finish_body(place_ref, *refs, others, has_sum, last):
    refs = list(refs)
    wide_ref = refs.pop()
    out_ref = refs.pop()
    plane = place_ref[0]
    total = refs.pop(0)[...] if has_sum else None
    groups, rows, size = refs[0].shape

    def gathered(attended_ref, slot):
        for g in range(groups):
            start = pl.multiple_of(lax.bitwise_xor(plane, g) * size, size)
            wide_ref[slot, :, pl.ds(start, size)] = attended_ref[g]

    @pl.when((pl.program_id(0) == 0) & (pl.program_id(1) == 0))
    def _():
        gathered(refs[0], 0)
        for m in range(others):
            gathered(refs[2 + 3 * m], 1 + m)

    def add(total, slot, weight):
        term = jnp.dot(wide_ref[slot], weight, preferred_element_type=f32)
        return term if total is None else total + term

    total = add(total, 0, refs[1][...])
    for m in range(others):
        near_ref, far_ref = refs[3 + 3 * m : 5 + 3 * m]
        total = add(total, 1 + m, jnp.where(pl.program_id(0) == 0, near_ref[...], far_ref[...]))
    if last:
        rounded = total.astype(bf16)
        out_ref[...] = jnp.dot(refs[-1][...], rounded, preferred_element_type=f32).astype(bf16)
    else:
        out_ref[...] = total


def column_split(out_width):
    return 2 if out_width % 256 == 0 else 1


def finish(place, total, attended, w_out, other_attended, other_weights, back, chunk, out_width):
    groups, rows, size = attended.shape
    split = column_split(out_width)
    half = out_width // split
    parts = column_split(half)
    tile = half // parts
    depth = groups * size
    column = lambda i, s, place: lax.bitwise_xor(place[1], i) * parts + s
    mine = lambda i, s, place: (0, column(i, s, place))
    own = lambda i, s, place: (chunk, place[2] * split * parts + column(i, s, place))
    near = lambda i, s, place: (chunk, jnp.where(i == 0, s, parts - 1))
    far = lambda i, s, place: (chunk, jnp.where(i == 0, 0, s))
    block_a = pl.BlockSpec((groups, rows, size), lambda i, s, place: (0, 0, 0))
    specs, operands = [], []
    if total is not None:
        specs.append(pl.BlockSpec((rows, tile), mine))
        operands.append(total)
    specs += [block_a, pl.BlockSpec((depth, tile), own)]
    operands += [attended, w_out]
    for other, weights in zip(other_attended, other_weights):
        specs += [block_a, pl.BlockSpec((depth, tile), near), pl.BlockSpec((depth, tile), far)]
        operands += [other, *weights]
    if back is not None:
        specs.append(pl.BlockSpec(back.shape, lambda i, s, place: (0, 0)))
        operands.append(back)
    last = back is not None
    count = 1 + len(other_attended)
    return pl.pallas_call(
        functools.partial(
            finish_body, others=len(other_attended), has_sum=total is not None, last=last
        ),
        grid_spec=pltpu.PrefetchScalarGridSpec(
            num_scalar_prefetch=1,
            grid=(split, parts),
            in_specs=specs,
            out_specs=pl.BlockSpec((rows, tile), mine),
            scratch_shapes=[pltpu.VMEM((count, rows, depth), bf16)],
        ),
        out_shape=jax.ShapeDtypeStruct((rows, out_width), bf16 if last else f32),
        compiler_params=params,
        cost_estimate=cost(
            2 * rows * depth * count * out_width, 2 * depth * count * out_width + 8 * rows * out_width
        ),
        name="finish",
    )(place, *operands)


def per_device(tokens, survive, norm_gain, w_qkv, qk_gain, w_out):
    heads = qk_gain.shape[1]
    shards, head_shards = lax.axis_size("seq"), lax.axis_size("head")
    out_width = w_out.shape[1] // head_shards
    split = column_split(out_width)
    half = out_width // split
    groups = math.gcd(heads & -heads, shards & -shards)
    ring = shards // groups
    chunks = heads // groups
    me, side = lax.axis_index("seq"), lax.axis_index("head")
    core = me % split
    place = jnp.stack([me // ring, core, side]).astype(jnp.int32)

    def swap(blocks):
        return [blocks[0]] + [flip(blocks[k], "seq", k * ring) for k in range(1, groups)]

    def after(values, blocks):
        return lax.optimization_barrier((values, blocks[1]))[0] if groups > 1 else values

    def everywhere(blocks):
        found = {0: jnp.concatenate(blocks) if groups > 1 else blocks[0]}
        mask = ring // 2
        while mask:
            for known in list(found):
                found[known | mask] = flip(found[known], "seq", mask)
            mask //= 2
        return [found[mask] for mask in range(ring)]

    normed, back, count = pack(tokens, survive, norm_gain)
    weights = jnp.transpose(w_qkv, (1, 0, 2))
    gains = jnp.transpose(qk_gain, (1, 0, 2))
    produce = functools.partial(project, place, count)

    keyval, query = produce(normed, weights, gains, (1, 2, 0), (0,), groups)
    keyval, query = swap(keyval), swap(query)
    keyvals, queries = [keyval], [(query, 0)]
    for chunk in range(1, chunks):
        keyval, _ = produce(after(normed, keyval), weights, gains, (1, 2), (chunk,), groups)
        keyval = swap(keyval)
        keyvals.append(keyval)
    if chunks > 1:
        rest = tuple(range(1, chunks))
        _, query = produce(after(normed, keyval), weights, gains, (0,), rest, groups)
        query = swap(query)
        queries += [(query, i) for i in range(chunks - 1)]

    other_weights = []
    for mask in range(1, head_shards):
        column = lax.bitwise_xor(side, mask) * out_width + core * half
        near = flip(lax.dynamic_slice(w_out, (0, column), (w_out.shape[0], half)), "head", mask)
        other_weights.append((near, flip(near, "seq", 1) if split == 2 else near))

    total = None
    for chunk in range(chunks):
        query, which = queries[chunk]
        attended = swap(attend(query, which, everywhere(keyvals[chunk]), shards))
        attended = jnp.concatenate(attended) if groups > 1 else attended[0]
        others = [flip(attended, "head", mask) for mask in range(1, head_shards)]
        total = finish(
            place,
            total,
            attended,
            w_out,
            others,
            other_weights,
            back if chunk == chunks - 1 else None,
            chunk,
            out_width,
        )
    return total


def solution(mesh):
    placed = (
        P("seq", None),
        P("seq"),
        P(),
        P(None, None, "head"),
        P(None, "head", None),
        P("head", None),
    )
    return jax.shard_map(
        per_device, mesh=mesh, in_specs=placed, out_specs=P("seq", "head"), check_vma=False
    )
```

time: 222 us -> 243 us (1.095)
  the two profiles are of different devices: /device:TPU:1 before, /device:TPU:0 now
where the time goes in v2:
time: 243 us; the launch traced here: 245 us
  Pallas kernels  107 us (44%)
  waiting for transfers between devices  75.8 us (31%)
  starting transfers between devices  46 us (19%)
  local copies, waits for them, and re-layouts  14.9 us (6%)
    ppermute x38, waiting for transfers between devices, flip(): return lax.ppermute(values, axis, [(i, i ^ mask) for i in range(size)])  75.8 us
    ppermute x38, starting transfers between devices, flip(): return lax.ppermute(values, axis, [(i, i ^ mask) for i in range(size)])  46 us
    pallas_call x4, Pallas kernels, project(): pl.pallas_call(functools.partial(project_body, kinds=kinds, chunks=chunks...  43.3 us
    pallas_call x3, Pallas kernels, attend(): pl.pallas_call(functools.partial(attend_body, groups=groups, sources=len(...  36.4 us
    pallas_call x3, Pallas kernels, finish(): pl.pallas_call(functools.partial(finish_body, others=len(other_attended),...  21.3 us
    unnamed x48, local copies, waits for them, and re-layouts  10.3 us
    pallas_call x1, Pallas kernels, pack(): pl.pallas_call(functools.partial(pack_body, rows=rows), grid=(positions /...  6.4 us
  transfers between devices with their start and end apart: 38, of which 15 were waited for; matrix products, arithmetic and copies ran while one was open for 4% of the time, Pallas kernels for 41%

profile of v2, /device:TPU:0, one launch (start us, length us, event | category | flops | bytes accessed | tf_op | source)
XLA Modules:
  0.0 245.0 jit_solution(13425402735507279781)
XLA Ops:
  0.0 3.2 %constant_dynamic-slice_fusion = bf16[1536,768]{1,0:T(8,128)(2,1)} fusion(bf16[1536,3072]{1,0:T(8,128)(2,1)} %refs_2_.3, s32[]{:T(128)S(6)} %select_n.16), kind=kLoop, calls=%fused_computation.25 | loop fusion | bytes 4718596 | tf_op jit(solution)/shard_map/dynamic_slice | solution.py:435
  3.2 2.9 %collective-permute-start.13 = (bf16[1536,768]{1,0:T(8,128)(2,1)}, bf16[1536,768]{1,0:T(8,128)(2,1)S(1)}, u32[]{:S(2)}, u32[]{:S(2)}) collective-permute-start(bf16[1536,768]{1,0:T(8,128)(2,1)} %constant_dynamic-slice_fusion), channel_id=1, source_target_pairs={{0,1},{1,0},{2,3},{3,2},{4,5},{5,4},{6,7},{7,6},{8,9},{9,8},{10,11... | collective-permute-start | bytes 7077896 | tf_op jit(solution)/shard_map/ppermute | solution.py:28
  6.8 6.4 %pack.1 = (bf16[384,3072]{1,0:T(8,128)(2,1)}, bf16[384,384]{1,0:T(8,128)(2,1)}, s32[1,1]{1,0:T(1,128)}) custom-call(s32[384]{0:T(512)} %survive_ref.1, bf16[384,3072]{1,0:T(8,128)(2,1)} %tokens_ref.1, f32[3072]{0:T(1024)} %gain_ref.1), custom_call_target="tpu_custom_call" | custom-call | flops 905969664 | bytes 4718592 | tf_op jit(solution)/shard_map/pack/pallas_call | solution.py:58
  13.2 13.5 %project.4 = (bf16[1,384,256]{2,1,0:T(8,128)(2,1)}, bf16[1,384,256]{2,1,0:T(8,128)(2,1)}, bf16[1,384,256]{2,1,0:T(8,128)(2,1)}, bf16[1,384,256]{2,1,0:T(8,128)(2...) custom-call(s32[3]{0:T(128)} %pad_add_fusion.place_ref, ...), custom_call_target="tpu_custom_call" | custom-call | flops 3623878656 | bytes 11796480 | tf_op jit(solution)/shard_map/project/pallas_call | solution.py:153
  26.7 1.6 collective-permute-start.3
  28.3 2.6 %collective-permute-start.4 = (bf16[1,384,256]{2,1,0:T(8,128)(2,1)}, bf16[1,384,256]{2,1,0:T(8,128)(2,1)S(1)}, u32[]{:S(2)}, u32[]{:S(2)}) collective-permute-start(bf16[1,384,256]{2,1,0:T(8,128)(2,1)} %get-tuple-element.51), channel_id=1, source_target_pairs={{0,16},{2,18},{4,20},{6,22},{8,24},{10,26},{12,28},{14,30},{16,0},... | collective-permute-start | bytes 589832 | tf_op jit(solution)/shard_map/ppermute | solution.py:28
  31.1 1.6 constant_dynamic-update-slice_fusion.3
  32.7 3.7 %collective-permute-done.3 = bf16[1,384,256]{2,1,0:T(8,128)(2,1)S(1)} collective-permute-done((bf16[1,384,256]{2,1,0:T(8,128)(2,1)}, bf16[1,384,256]{2,1,0:T(8,128)(2,1)S(1)}, u32[]{:S(2)}, u32[]{:S(2)}) %collective-permute-start.3) | collective-permute-done | bytes 196640 | tf_op jit(solution)/shard_map/ppermute | solution.py:28
  37.1 8.6 %collective-permute-done.4 = bf16[1,384,256]{2,1,0:T(8,128)(2,1)S(1)} collective-permute-done((bf16[1,384,256]{2,1,0:T(8,128)(2,1)}, bf16[1,384,256]{2,1,0:T(8,128)(2,1)S(1)}, u32[]{:S(2)}, u32[]{:S(2)}) %collective-permute-start.4) | collective-permute-done | bytes 196640 | tf_op jit(solution)/shard_map/ppermute | solution.py:28
  47.0 1.5 collective-permute-start.7
  48.5 9.7 %project.5 = (bf16[1,384,256]{2,1,0:T(8,128)(2,1)}, bf16[1,384,256]{2,1,0:T(8,128)(2,1)}, bf16[1,384,256]{2,1,0:T(8,128)(2,1)}, bf16[1,384,256]{2,1,0:T(8,128)(2,1)}) custom-call(s32[3]{0:T(128)} %pad_add_fusion.place_ref, s32[1,1]{1,0:T(1,128)} %get-tuple-element.43.count_ref, bf16[384,3072]{1,0:T(8,128)(2,1)} %get-tuple-element.61.normed_ref, ...), custom_call_target="tpu_custom_call" | custom-call | flops 2415919104 | bytes 8650752 | tf_op jit(solution)/shard_map/project/pallas_call | solution.py:153
  58.2 2.4 collective-permute-start.15
  60.7 2.9 %collective-permute-start.20 = (bf16[1,384,256]{2,1,0:T(8,128)(2,1)}, bf16[1,384,256]{2,1,0:T(8,128)(2,1)S(1)}, u32[]{:S(2)}, u32[]{:S(2)}) collective-permute-start(bf16[1,384,256]{2,1,0:T(8,128)(2,1)} %get-tuple-element.67), channel_id=1, source_target_pairs={{0,16},{2,18},{4,20},{6,22},{8,24},{10,26},{12,28},{14,30},{16,0},... | collective-permute-start | bytes 589832 | tf_op jit(solution)/shard_map/ppermute | solution.py:28
  63.6 0.9 constant_dynamic-update-slice_fusion.11
  64.6 3.5 %collective-permute-done.15 = bf16[1,384,256]{2,1,0:T(8,128)(2,1)S(1)} collective-permute-done((bf16[1,384,256]{2,1,0:T(8,128)(2,1)}, bf16[1,384,256]{2,1,0:T(8,128)(2,1)S(1)}, u32[]{:S(2)}, u32[]{:S(2)}) %collective-permute-start.15) | collective-permute-done | bytes 196640 | tf_op jit(solution)/shard_map/ppermute | solution.py:28
  68.1 2.5 %collective-permute-start.21 = (bf16[1,384,256]{2,1,0:T(8,128)(2,1)}, bf16[1,384,256]{2,1,0:T(8,128)(2,1)S(1)}, u32[]{:S(2)}, u32[]{:S(2)}) collective-permute-start(bf16[1,384,256]{2,1,0:T(8,128)(2,1)} %get-tuple-element.68), channel_id=1, source_target_pairs={{0,24},{2,26},{4,28},{6,30},{8,16},{10,18},{12,20},{14,22},{16,8},... | collective-permute-start | bytes 589832 | tf_op jit(solution)/shard_map/ppermute | solution.py:28
  70.6 9.8 %project.6 = (bf16[1,384,256]{2,1,0:T(8,128)(2,1)}, bf16[1,384,256]{2,1,0:T(8,128)(2,1)}, bf16[1,384,256]{2,1,0:T(8,128)(2,1)}, bf16[1,384,256]{2,1,0:T(8,128)(2,1)}) custom-call(s32[3]{0:T(128)} %pad_add_fusion.place_ref, s32[1,1]{1,0:T(1,128)} %get-tuple-element.43.count_ref, bf16[384,3072]{1,0:T(8,128)(2,1)} %get-tuple-element.61.normed_ref, ...), custom_call_target="tpu_custom_call" | custom-call | flops 2415919104 | bytes 8650752 | tf_op jit(solution)/shard_map/project/pallas_call | solution.py:153
  80.4 2.0 collective-permute-start.29
  82.4 4.5 %collective-permute-start.1 = (bf16[1,384,128]{2,1,0:T(8,128)(2,1)}, bf16[1,384,128]{2,1,0:T(8,128)(2,1)S(1)}, u32[]{:S(2)}, u32[]{:S(2)}) collective-permute-start(bf16[1,384,128]{2,1,0:T(8,128)(2,1)} %get-tuple-element.47), channel_id=1, source_target_pairs={{0,16},{2,18},{4,20},{6,22},{8,24},{10,26},{12,28},{14,30},{16,0},... | collective-permute-start | bytes 294920 | tf_op jit(solution)/shard_map/ppermute | solution.py:28
  86.9 1.5 collective-permute-done.16
  88.5 2.2 collective-permute-start.2
  90.7 5.2 %collective-permute-done.1.refs_2_ = bf16[1,384,128]{2,1,0:T(8,128)(2,1)S(1)} collective-permute-done((bf16[1,384,128]{2,1,0:T(8,128)(2,1)}, bf16[1,384,128]{2,1,0:T(8,128)(2,1)S(1)}, u32[]{:S(2)}, u32[]{:S(2)}) %collective-permute-start.1) | collective-permute-done | bytes 98336 | tf_op jit(solution)/shard_map/ppermute | solution.py:28
  96.6 1.9 collective-permute-start.30
  98.9 10.4 %project.7 = (bf16[2,384,128]{2,1,0:T(8,128)(2,1)}, bf16[2,384,128]{2,1,0:T(8,128)(2,1)}, bf16[2,384,128]{2,1,0:T(8,128)(2,1)}, bf16[2,384,128]{2,1,0:T(8,128)(2,1)}) custom-call(s32[3]{0:T(128)} %pad_add_fusion.place_ref, s32[1,1]{1,0:T(1,128)} %get-tuple-element.43.count_ref, bf16[384,3072]{1,0:T(8,128)(2,1)} %get-tuple-element.61.normed_ref, ...), custom_call_target="tpu_custom_call" | custom-call | flops 2415919104 | bytes 8650752 | tf_op jit(solution)/shard_map/project/pallas_call | solution.py:153
  111.4 5.5 %collective-permute-done.17.refs_1_ = bf16[2,384,128]{2,1,0:T(8,128)(2,1)S(1)} collective-permute-done((bf16[2,384,128]{2,1,0:T(8,128)(2,1)}, bf16[2,384,128]{2,1,0:T(8,128)(2,1)S(1)}, u32[]{:S(2)}, u32[]{:S(2)}) %collective-permute-start.17) | collective-permute-done | bytes 196640 | tf_op jit(solution)/shard_map/ppermute | solution.py:28
  116.9 1.2 collective-permute-start.18
  119.5 9.4 %collective-permute-done.18.refs_2_ = bf16[2,384,128]{2,1,0:T(8,128)(2,1)S(1)} collective-permute-done((bf16[2,384,128]{2,1,0:T(8,128)(2,1)}, bf16[2,384,128]{2,1,0:T(8,128)(2,1)S(1)}, u32[]{:S(2)}, u32[]{:S(2)}) %collective-permute-start.18) | collective-permute-done | bytes 196640 | tf_op jit(solution)/shard_map/ppermute | solution.py:28
  128.9 1.6 collective-permute-start.32
  131.1 1.9 collective-permute-start.19
  133.0 12.2 %attend.3 = (bf16[1,384,128]{2,1,0:T(8,128)(2,1)}, bf16[1,384,128]{2,1,0:T(8,128)(2,1)}, bf16[1,384,128]{2,1,0:T(8,128)(2,1)}, bf16[1,384,128]{2,1,0:T(8,128)(2,1)}) custom-call(bf16[1,384,128]{2,1,0:T(8,128)(2,1)} %get-tuple-element.45.refs_0_, bf16[1,384,128]{2,1,0:T(8,128)(2,1)} %copy-done.10, bf16[1,384,128]{2,1,0:T(8,128)(2,1)} %copy-done.11, ...), custom_call_target="tpu_custom_call" | custom-call | flops 2415919104 | bytes 3145728 | tf_op jit(solution)/shard_map/attend/pallas_call | solution.py:271
  146.2 4.7 %collective-permute-done.9 = bf16[1,384,128]{2,1,0:T(8,128)(2,1)S(1)} collective-permute-done((bf16[1,384,128]{2,1,0:T(8,128)(2,1)}, bf16[1,384,128]{2,1,0:T(8,128)(2,1)S(1)}, u32[]{:S(2)}, u32[]{:S(2)}) %collective-permute-start.9) | collective-permute-done | bytes 98336 | tf_op jit(solution)/shard_map/ppermute | solution.py:28
  151.6 6.8 %collective-permute-done.10 = bf16[1,384,128]{2,1,0:T(8,128)(2,1)S(1)} collective-permute-done((bf16[1,384,128]{2,1,0:T(8,128)(2,1)}, bf16[1,384,128]{2,1,0:T(8,128)(2,1)S(1)}, u32[]{:S(2)}, u32[]{:S(2)}) %collective-permute-start.10) | collective-permute-done | bytes 98336 | tf_op jit(solution)/shard_map/ppermute | solution.py:28
  158.4 1.9 collective-permute-start.11
  160.4 4.6 %collective-permute-done.11 = bf16[1,384,128]{2,1,0:T(8,128)(2,1)S(1)} collective-permute-done((bf16[1,384,128]{2,1,0:T(8,128)(2,1)}, bf16[1,384,128]{2,1,0:T(8,128)(2,1)S(1)}, u32[]{:S(2)}, u32[]{:S(2)}) %collective-permute-start.11) | collective-permute-done | bytes 98336 | tf_op jit(solution)/shard_map/ppermute | solution.py:28
  165.7 12.1 %attend.4 = (bf16[1,384,128]{2,1,0:T(8,128)(2,1)}, bf16[1,384,128]{2,1,0:T(8,128)(2,1)}, bf16[1,384,128]{2,1,0:T(8,128)(2,1)}, bf16[1,384,128]{2,1,0:T(8,128)(2,1)}) custom-call(bf16[2,384,128]{2,1,0:T(8,128)(2,1)} %get-tuple-element.62.refs_0_, bf16[2,384,128]{2,1,0:T(8,128)(2,1)} %copy-done.7, bf16[2,384,128]{2,1,0:T(8,128)(2,1)} %copy-done.8, ...), custom_call_target="tpu_custom_call" | custom-call | flops 2415919104 | bytes 3145728 | tf_op jit(solution)/shard_map/attend/pallas_call | solution.py:271
  178.7 4.9 %collective-permute-done.25 = bf16[1,384,128]{2,1,0:T(8,128)(2,1)S(1)} collective-permute-done((bf16[1,384,128]{2,1,0:T(8,128)(2,1)}, bf16[1,384,128]{2,1,0:T(8,128)(2,1)S(1)}, u32[]{:S(2)}, u32[]{:S(2)}) %collective-permute-start.25) | collective-permute-done | bytes 98336 | tf_op jit(solution)/shard_map/ppermute | solution.py:28
  183.9 6.6 %collective-permute-done.26 = bf16[1,384,128]{2,1,0:T(8,128)(2,1)S(1)} collective-permute-done((bf16[1,384,128]{2,1,0:T(8,128)(2,1)}, bf16[1,384,128]{2,1,0:T(8,128)(2,1)S(1)}, u32[]{:S(2)}, u32[]{:S(2)}) %collective-permute-start.26) | collective-permute-done | bytes 98336 | tf_op jit(solution)/shard_map/ppermute | solution.py:28
  190.6 2.1 collective-permute-start.27
  192.7 4.5 %collective-permute-done.27 = bf16[1,384,128]{2,1,0:T(8,128)(2,1)S(1)} collective-permute-done((bf16[1,384,128]{2,1,0:T(8,128)(2,1)}, bf16[1,384,128]{2,1,0:T(8,128)(2,1)S(1)}, u32[]{:S(2)}, u32[]{:S(2)}) %collective-permute-start.27) | collective-permute-done | bytes 98336 | tf_op jit(solution)/shard_map/ppermute | solution.py:28
  197.2 1.7 collective-permute-start.28
  198.9 12.1 %attend.5 = (bf16[1,384,128]{2,1,0:T(8,128)(2,1)}, bf16[1,384,128]{2,1,0:T(8,128)(2,1)}, bf16[1,384,128]{2,1,0:T(8,128)(2,1)}, bf16[1,384,128]{2,1,0:T(8,128)(2,1)}) custom-call(bf16[2,384,128]{2,1,0:T(8,128)(2,1)} %get-tuple-element.62.refs_0_, bf16[2,384,128]{2,1,0:T(8,128)(2,1)} %copy-done.7, bf16[2,384,128]{2,1,0:T(8,128)(2,1)} %copy-done.8, ...), custom_call_target="tpu_custom_call" | custom-call | flops 2415919104 | bytes 3145728 | tf_op jit(solution)/shard_map/attend/pallas_call | solution.py:271
  211.0 2.5 %collective-permute-start.35 = (bf16[1,384,128]{2,1,0:T(8,128)(2,1)}, bf16[1,384,128]{2,1,0:T(8,128)(2,1)S(1)}, u32[]{:S(2)}, u32[]{:S(2)}) collective-permute-start(bf16[1,384,128]{2,1,0:T(8,128)(2,1)} %get-tuple-element.78), channel_id=1, source_target_pairs={{0,16},{2,18},{4,20},{6,22},{8,24},{10,26},{12,28},{14,30},{16,0},... | collective-permute-start | bytes 294920 | tf_op jit(solution)/shard_map/ppermute | solution.py:28
  214.4 1.5 collective-permute-done.34
  215.8 1.9 collective-permute-start.36
  217.8 4.7 %collective-permute-done.36 = bf16[1,384,128]{2,1,0:T(8,128)(2,1)S(1)} collective-permute-done((bf16[1,384,128]{2,1,0:T(8,128)(2,1)}, bf16[1,384,128]{2,1,0:T(8,128)(2,1)S(1)}, u32[]{:S(2)}, u32[]{:S(2)}) %collective-permute-start.36) | collective-permute-done | bytes 98336 | tf_op jit(solution)/shard_map/ppermute | solution.py:28
  223.7 6.5 %finish.3.refs_0_ = f32[384,1536]{1,0:T(8,128)} custom-call(s32[3]{0:T(128)} %pad_add_fusion.place_ref, bf16[4,384,128]{2,1,0:T(8,128)(2,1)} %copy-done.2, bf16[1536,3072]{1,0:T(8,128)(2,1)} %refs_2_.3, bf16[4,384,128]{2,1,0:T(8,128)(2,1)} %copy-done.4, bf16[1536,768]{1,0:T(8,128)(2,1)} %copy-done, bf16[1536,768]{1,0:T(8,128)(2,1)} %collective-permute-done.14.refs_4_.refs_5_), custom_call_target="tpu_custom_call" | custom-call | flops 1207959552 | bytes 7864320 | tf_op jit(solution)/shard_map/finish/pallas_call | solution.py:366
  230.3 7.0 %finish.4.refs_0_ = f32[384,1536]{1,0:T(8,128)} custom-call(s32[3]{0:T(128)} %pad_add_fusion.place_ref, f32[384,1536]{1,0:T(8,128)} %finish.3.refs_0_, bf16[4,384,128]{2,1,0:T(8,128)(2,1)} %copy-done.3, bf16[1536,3072]{1,0:T(8,128)(2,1)} %refs_2_.3, bf16[4,384,128]{2,1,0:T(8,128)(2,1)} %collective-permute-done.28.refs_3_, bf16[1536,768]{1,0:T(8,128)(2,1)} %copy-done, ...), custom_call_target="tpu_custom_call" | custom-call | flops 1207959552 | bytes 7864320 | tf_op jit(solution)/shard_map/finish/pallas_call | solution.py:366
  237.3 7.7 %finish.5 = bf16[384,1536]{1,0:T(8,128)(2,1)} custom-call(s32[3]{0:T(128)} %pad_add_fusion.place_ref, f32[384,1536]{1,0:T(8,128)} %finish.4.refs_0_, bf16[4,384,128]{2,1,0:T(8,128)(2,1)} %copy-done.1, bf16[1536,3072]{1,0:T(8,128)(2,1)} %refs_2_.3, bf16[4,384,128]{2,1,0:T(8,128)(2,1)} %collective-permute-done.37.refs_3_, bf16[1536,768]{1,0:T(8,128)(2,1)} %copy-done, ...), custom_call_target="tpu_custom_call" | custom-call | flops 1207959552 | bytes 7864320 | tf_op jit(solution)/shard_map/finish/pallas_call | solution.py:366
  (95 shorter events, 14.2 us)
Async XLA Ops:
  3.2 127.3 %collective-permute-start.13 = (bf16[1536,768]{1,0:T(8,128)(2,1)}, bf16[1536,768]{1,0:T(8,128)(2,1)S(1)}, u32[]{:S(2)}, u32[]{:S(2)}) collective-permute-start(bf16[1536,768]{1,0:T(8,128)(2,1)} %constant_dynamic-slice_fusion), channel_id=1, source_target_pairs={{0,1},{1,0},{2,3},{3,2},{4,5},{5,4},{6,7},{7,6},{8,9},{9,8},{10,11... | collective-permute-start | bytes 7077896 | tf_op jit(solution)/shard_map/ppermute | solution.py:28
  26.7 9.7 %collective-permute-start.3 = (bf16[1,384,256]{2,1,0:T(8,128)(2,1)}, bf16[1,384,256]{2,1,0:T(8,128)(2,1)S(1)}, u32[]{:S(2)}, u32[]{:S(2)}) collective-permute-start(bf16[1,384,256]{2,1,0:T(8,128)(2,1)} %get-tuple-element.50), channel_id=1, source_target_pairs={{0,8},{2,10},{4,12},{6,14},{8,0},{10,2},{12,4},{14,6},{16,24},{18,... | collective-permute-start | bytes 589832 | tf_op jit(solution)/shard_map/ppermute | solution.py:28
  28.3 17.4 %collective-permute-start.4 = (bf16[1,384,256]{2,1,0:T(8,128)(2,1)}, bf16[1,384,256]{2,1,0:T(8,128)(2,1)S(1)}, u32[]{:S(2)}, u32[]{:S(2)}) collective-permute-start(bf16[1,384,256]{2,1,0:T(8,128)(2,1)} %get-tuple-element.51), channel_id=1, source_target_pairs={{0,16},{2,18},{4,20},{6,22},{8,24},{10,26},{12,28},{14,30},{16,0},... | collective-permute-start | bytes 589832 | tf_op jit(solution)/shard_map/ppermute | solution.py:28
  30.8 15.5 %collective-permute-start.5 = (bf16[1,384,256]{2,1,0:T(8,128)(2,1)}, bf16[1,384,256]{2,1,0:T(8,128)(2,1)S(1)}, u32[]{:S(2)}, u32[]{:S(2)}) collective-permute-start(bf16[1,384,256]{2,1,0:T(8,128)(2,1)} %get-tuple-element.52), channel_id=1, source_target_pairs={{0,24},{2,26},{4,28},{6,30},{8,16},{10,18},{12,20},{14,22},{16,8},... | collective-permute-start | bytes 589832 | tf_op jit(solution)/shard_map/ppermute | solution.py:28
  47.0 13.6 %copy-start.14 = (bf16[1,384,128]{2,1,0:T(8,128)(2,1)S(1)}, bf16[1,384,128]{2,1,0:T(8,128)(2,1)}, u32[]{:S(2)}) copy-start(bf16[1,384,128]{2,1,0:T(8,128)(2,1)} %get-tuple-element.46) | copy-start | bytes 294916
  47.0 51.9 %collective-permute-start.7 = (bf16[4,384,256]{2,1,0:T(8,128)(2,1)}, bf16[4,384,256]{2,1,0:T(8,128)(2,1)}, u32[]{:S(2)}, u32[]{:S(2)}) collective-permute-start(bf16[4,384,256]{2,1,0:T(8,128)(2,1)} %constant_dynamic-update-slice_fusion.refs_4_), channel_id=1, source_target_pairs={{0,4},{2,6},{4,0},{6,2},{8,12},{10,14},{12,8},{14,10},{16,20},{18,... | collective-permute-start | bytes 2359304 | tf_op jit(solution)/shard_map/ppermute | solution.py:28
  58.2 9.9 %collective-permute-start.15 = (bf16[1,384,256]{2,1,0:T(8,128)(2,1)}, bf16[1,384,256]{2,1,0:T(8,128)(2,1)S(1)}, u32[]{:S(2)}, u32[]{:S(2)}) collective-permute-start(bf16[1,384,256]{2,1,0:T(8,128)(2,1)} %get-tuple-element.58), channel_id=1, source_target_pairs={{0,8},{2,10},{4,12},{6,14},{8,0},{10,2},{12,4},{14,6},{16,24},{18,... | collective-permute-start | bytes 589832 | tf_op jit(solution)/shard_map/ppermute | solution.py:28
  60.6 19.7 %collective-permute-start = (bf16[1,384,128]{2,1,0:T(8,128)(2,1)S(1)}, bf16[1,384,128]{2,1,0:T(8,128)(2,1)S(1)}, u32[]{:S(2)}, u32[]{:S(2)}) collective-permute-start(bf16[1,384,128]{2,1,0:T(8,128)(2,1)S(1)} %copy-done.14), channel_id=1, source_target_pairs={{0,8},{2,10},{4,12},{6,14},{8,0},{10,2},{12,4},{14,6},{16,24},{18,... | collective-permute-start | bytes 294920 | tf_op jit(solution)/shard_map/ppermute | solution.py:28
  60.7 19.7 %collective-permute-start.20 = (bf16[1,384,256]{2,1,0:T(8,128)(2,1)}, bf16[1,384,256]{2,1,0:T(8,128)(2,1)S(1)}, u32[]{:S(2)}, u32[]{:S(2)}) collective-permute-start(bf16[1,384,256]{2,1,0:T(8,128)(2,1)} %get-tuple-element.67), channel_id=1, source_target_pairs={{0,16},{2,18},{4,20},{6,22},{8,24},{10,26},{12,28},{14,30},{16,0},... | collective-permute-start | bytes 589832 | tf_op jit(solution)/shard_map/ppermute | solution.py:28
  68.1 20.4 %copy-start.12 = (bf16[1,384,128]{2,1,0:T(8,128)(2,1)S(1)}, bf16[1,384,128]{2,1,0:T(8,128)(2,1)}, u32[]{:S(2)}) copy-start(bf16[1,384,128]{2,1,0:T(8,128)(2,1)} %get-tuple-element.48) | copy-start | bytes 294916
  68.1 14.3 %collective-permute-start.21 = (bf16[1,384,256]{2,1,0:T(8,128)(2,1)}, bf16[1,384,256]{2,1,0:T(8,128)(2,1)S(1)}, u32[]{:S(2)}, u32[]{:S(2)}) collective-permute-start(bf16[1,384,256]{2,1,0:T(8,128)(2,1)} %get-tuple-element.68), channel_id=1, source_target_pairs={{0,24},{2,26},{4,28},{6,30},{8,16},{10,18},{12,20},{14,22},{16,8},... | collective-permute-start | bytes 589832 | tf_op jit(solution)/shard_map/ppermute | solution.py:28
  80.3 29.0 %copy-start.10 = (bf16[1,384,128]{2,1,0:T(8,128)(2,1)}, bf16[1,384,128]{2,1,0:T(8,128)(2,1)S(1)}, u32[]{:S(2)}) copy-start(bf16[1,384,128]{2,1,0:T(8,128)(2,1)S(1)} %collective-permute-done.refs_1_) | copy-start | bytes 294916
  80.3 8.2 %collective-permute-start.16 = (bf16[1,384,256]{2,1,0:T(8,128)(2,1)}, bf16[1,384,256]{2,1,0:T(8,128)(2,1)S(1)}, u32[]{:S(2)}, u32[]{:S(2)}) collective-permute-start(bf16[1,384,256]{2,1,0:T(8,128)(2,1)} %get-tuple-element.60), channel_id=1, source_target_pairs={{0,8},{2,10},{4,12},{6,14},{8,0},{10,2},{12,4},{14,6},{16,24},{18,... | collective-permute-start | bytes 589832 | tf_op jit(solution)/shard_map/ppermute | solution.py:28
  80.4 18.1 %collective-permute-start.29 = (bf16[1,384,256]{2,1,0:T(8,128)(2,1)}, bf16[1,384,256]{2,1,0:T(8,128)(2,1)S(1)}, u32[]{:S(2)}, u32[]{:S(2)}) collective-permute-start(bf16[1,384,256]{2,1,0:T(8,128)(2,1)} %get-tuple-element.74), channel_id=1, source_target_pairs={{0,16},{2,18},{4,20},{6,22},{8,24},{10,26},{12,28},{14,30},{16,0},... | collective-permute-start | bytes 589832 | tf_op jit(solution)/shard_map/ppermute | solution.py:28
  82.4 13.5 %collective-permute-start.1 = (bf16[1,384,128]{2,1,0:T(8,128)(2,1)}, bf16[1,384,128]{2,1,0:T(8,128)(2,1)S(1)}, u32[]{:S(2)}, u32[]{:S(2)}) collective-permute-start(bf16[1,384,128]{2,1,0:T(8,128)(2,1)} %get-tuple-element.47), channel_id=1, source_target_pairs={{0,16},{2,18},{4,20},{6,22},{8,24},{10,26},{12,28},{14,30},{16,0},... | collective-permute-start | bytes 294920 | tf_op jit(solution)/shard_map/ppermute | solution.py:28
  88.5 7.4 %collective-permute-start.2 = (bf16[1,384,128]{2,1,0:T(8,128)(2,1)S(1)}, bf16[1,384,128]{2,1,0:T(8,128)(2,1)S(1)}, u32[]{:S(2)}, u32[]{:S(2)}) collective-permute-start(bf16[1,384,128]{2,1,0:T(8,128)(2,1)S(1)} %copy-done.12), channel_id=1, source_target_pairs={{0,24},{2,26},{4,28},{6,30},{8,16},{10,18},{12,20},{14,22},{16,8},... | collective-permute-start | bytes 294920 | tf_op jit(solution)/shard_map/ppermute | solution.py:28
  90.6 39.8 %copy-start.6 = (bf16[4,384,256]{2,1,0:T(8,128)(2,1)}, bf16[4,384,256]{2,1,0:T(8,128)(2,1)S(1)}, u32[]{:S(2)}) copy-start(bf16[4,384,256]{2,1,0:T(8,128)(2,1)S(1)} %constant_dynamic-update-slice_fusion.8.refs_4_) | copy-start | bytes 2359300
  95.9 34.6 %collective-permute-start.6 = (bf16[4,384,256]{2,1,0:T(8,128)(2,1)}, bf16[4,384,256]{2,1,0:T(8,128)(2,1)}, u32[]{:S(2)}, u32[]{:S(2)}) collective-permute-start(bf16[4,384,256]{2,1,0:T(8,128)(2,1)} %constant_dynamic-update-slice_fusion.refs_4_), channel_id=1, source_target_pairs={{0,2},{2,0},{4,6},{6,4},{8,10},{10,8},{12,14},{14,12},{16,18},{18,... | collective-permute-start | bytes 2359304 | tf_op jit(solution)/shard_map/ppermute | solution.py:28
  96.6 13.5 %copy-start.5 = (bf16[1,384,256]{2,1,0:T(8,128)(2,1)S(1)}, bf16[1,384,256]{2,1,0:T(8,128)(2,1)}, u32[]{:S(2)}) copy-start(bf16[1,384,256]{2,1,0:T(8,128)(2,1)} %get-tuple-element.73) | copy-start | bytes 589828
  96.6 12.7 %collective-permute-start.30 = (bf16[1,384,256]{2,1,0:T(8,128)(2,1)}, bf16[1,384,256]{2,1,0:T(8,128)(2,1)S(1)}, u32[]{:S(2)}, u32[]{:S(2)}) collective-permute-start(bf16[1,384,256]{2,1,0:T(8,128)(2,1)} %get-tuple-element.75), channel_id=1, source_target_pairs={{0,24},{2,26},{4,28},{6,30},{8,16},{10,18},{12,20},{14,22},{16,8},... | collective-permute-start | bytes 589832 | tf_op jit(solution)/shard_map/ppermute | solution.py:28
  98.5 32.5 %collective-permute-start.23 = (bf16[4,384,256]{2,1,0:T(8,128)(2,1)S(1)}, bf16[4,384,256]{2,1,0:T(8,128)(2,1)}, u32[]{:S(2)}, u32[]{:S(2)}) collective-permute-start(bf16[4,384,256]{2,1,0:T(8,128)(2,1)S(1)} %constant_dynamic-update-slice_fusion.8.refs_4_), channel_id=1, source_target_pairs={{0,4},{2,6},{4,0},{6,2},{8,12},{10,14},{12,8},{14,10},{16,20},{18,... | collective-permute-start | bytes 2359304 | tf_op jit(solution)/shard_map/ppermute | solution.py:28
  98.9 32.1 %collective-permute-start.8 = (bf16[4,384,256]{2,1,0:T(8,128)(2,1)}, bf16[4,384,256]{2,1,0:T(8,128)(2,1)}, u32[]{:S(2)}, u32[]{:S(2)}) collective-permute-start(bf16[4,384,256]{2,1,0:T(8,128)(2,1)} %collective-permute-done.7.refs_6_), channel_id=1, source_target_pairs={{0,2},{2,0},{4,6},{6,4},{8,10},{10,8},{12,14},{14,12},{16,18},{18,... | collective-permute-start | bytes 2359304 | tf_op jit(solution)/shard_map/ppermute | solution.py:28
  109.3 7.6 %collective-permute-start.17 = (bf16[2,384,128]{2,1,0:T(8,128)(2,1)}, bf16[2,384,128]{2,1,0:T(8,128)(2,1)S(1)}, u32[]{:S(2)}, u32[]{:S(2)}) collective-permute-start(bf16[2,384,128]{2,1,0:T(8,128)(2,1)} %get-tuple-element.63), channel_id=1, source_target_pairs={{0,8},{2,10},{4,12},{6,14},{8,0},{10,2},{12,4},{14,6},{16,24},{18,... | collective-permute-start | bytes 589832 | tf_op jit(solution)/shard_map/ppermute | solution.py:28
  116.9 14.1 %copy-start.7 = (bf16[2,384,128]{2,1,0:T(8,128)(2,1)}, bf16[2,384,128]{2,1,0:T(8,128)(2,1)S(1)}, u32[]{:S(2)}) copy-start(bf16[2,384,128]{2,1,0:T(8,128)(2,1)S(1)} %collective-permute-done.17.refs_1_) | copy-start | bytes 589828
  116.9 12.0 %collective-permute-start.18 = (bf16[2,384,128]{2,1,0:T(8,128)(2,1)}, bf16[2,384,128]{2,1,0:T(8,128)(2,1)S(1)}, u32[]{:S(2)}, u32[]{:S(2)}) collective-permute-start(bf16[2,384,128]{2,1,0:T(8,128)(2,1)} %get-tuple-element.64), channel_id=1, source_target_pairs={{0,16},{2,18},{4,20},{6,22},{8,24},{10,26},{12,28},{14,30},{16,0},... | collective-permute-start | bytes 589832 | tf_op jit(solution)/shard_map/ppermute | solution.py:28
  128.9 16.4 %copy-start.8 = (bf16[2,384,128]{2,1,0:T(8,128)(2,1)}, bf16[2,384,128]{2,1,0:T(8,128)(2,1)S(1)}, u32[]{:S(2)}) copy-start(bf16[2,384,128]{2,1,0:T(8,128)(2,1)S(1)} %collective-permute-done.18.refs_2_) | copy-start | bytes 589828
  128.9 31.4 %collective-permute-start.32 = (bf16[4,384,256]{2,1,0:T(8,128)(2,1)}, bf16[4,384,256]{2,1,0:T(8,128)(2,1)}, u32[]{:S(2)}, u32[]{:S(2)}) collective-permute-start(bf16[4,384,256]{2,1,0:T(8,128)(2,1)} %constant_dynamic-update-slice_fusion.16.refs_4_), channel_id=1, source_target_pairs={{0,4},{2,6},{4,0},{6,2},{8,12},{10,14},{12,8},{14,10},{16,20},{18,... | collective-permute-start | bytes 2359304 | tf_op jit(solution)/shard_map/ppermute | solution.py:28
  130.5 14.8 %copy-start = (bf16[1536,768]{1,0:T(8,128)(2,1)}, bf16[1536,768]{1,0:T(8,128)(2,1)S(1)}, u32[]{:S(2)}) copy-start(bf16[1536,768]{1,0:T(8,128)(2,1)S(1)} %collective-permute-done.13.refs_3_.refs_4_) | copy-start | bytes 7077892
  130.5 92.5 %collective-permute-start.14 = (bf16[1536,768]{1,0:T(8,128)(2,1)S(1)}, bf16[1536,768]{1,0:T(8,128)(2,1)}, u32[]{:S(2)}, u32[]{:S(2)}) collective-permute-start(bf16[1536,768]{1,0:T(8,128)(2,1)S(1)} %collective-permute-done.13.refs_3_.refs_4_), channel_id=1, source_target_pairs={{0,2},{2,0},{4,6},{6,4},{8,10},{10,8},{12,14},{14,12},{16,18},{18,... | collective-permute-start | bytes 7077896 | tf_op jit(solution)/shard_map/ppermute | solution.py:28
  130.5 34.6 %collective-permute-start.22 = (bf16[4,384,256]{2,1,0:T(8,128)(2,1)S(1)}, bf16[4,384,256]{2,1,0:T(8,128)(2,1)}, u32[]{:S(2)}, u32[]{:S(2)}) collective-permute-start(bf16[4,384,256]{2,1,0:T(8,128)(2,1)S(1)} %constant_dynamic-update-slice_fusion.8.refs_4_), channel_id=1, source_target_pairs={{0,2},{2,0},{4,6},{6,4},{8,10},{10,8},{12,14},{14,12},{16,18},{18,... | collective-permute-start | bytes 2359304 | tf_op jit(solution)/shard_map/ppermute | solution.py:28
  131.0 34.7 %collective-permute-start.24 = (bf16[4,384,256]{2,1,0:T(8,128)(2,1)}, bf16[4,384,256]{2,1,0:T(8,128)(2,1)}, u32[]{:S(2)}, u32[]{:S(2)}) collective-permute-start(bf16[4,384,256]{2,1,0:T(8,128)(2,1)} %collective-permute-done.23.refs_6_), channel_id=1, source_target_pairs={{0,2},{2,0},{4,6},{6,4},{8,10},{10,8},{12,14},{14,12},{16,18},{18,... | collective-permute-start | bytes 2359304 | tf_op jit(solution)/shard_map/ppermute | solution.py:28
  131.1 14.2 %collective-permute-start.19 = (bf16[2,384,128]{2,1,0:T(8,128)(2,1)}, bf16[2,384,128]{2,1,0:T(8,128)(2,1)S(1)}, u32[]{:S(2)}, u32[]{:S(2)}) collective-permute-start(bf16[2,384,128]{2,1,0:T(8,128)(2,1)} %get-tuple-element.65), channel_id=1, source_target_pairs={{0,24},{2,26},{4,28},{6,30},{8,16},{10,18},{12,20},{14,22},{16,8},... | collective-permute-start | bytes 589832 | tf_op jit(solution)/shard_map/ppermute | solution.py:28
  145.2 20.5 %copy-start.9 = (bf16[2,384,128]{2,1,0:T(8,128)(2,1)}, bf16[2,384,128]{2,1,0:T(8,128)(2,1)S(1)}, u32[]{:S(2)}) copy-start(bf16[2,384,128]{2,1,0:T(8,128)(2,1)S(1)} %collective-permute-done.19.refs_3_) | copy-start | bytes 589828
  145.3 5.7 %collective-permute-start.9 = (bf16[1,384,128]{2,1,0:T(8,128)(2,1)}, bf16[1,384,128]{2,1,0:T(8,128)(2,1)S(1)}, u32[]{:S(2)}, u32[]{:S(2)}) collective-permute-start(bf16[1,384,128]{2,1,0:T(8,128)(2,1)} %get-tuple-element.54), channel_id=1, source_target_pairs={{0,8},{2,10},{4,12},{6,14},{8,0},{10,2},{12,4},{14,6},{16,24},{18,... | collective-permute-start | bytes 294920 | tf_op jit(solution)/shard_map/ppermute | solution.py:28
  150.9 7.5 %collective-permute-start.10 = (bf16[1,384,128]{2,1,0:T(8,128)(2,1)}, bf16[1,384,128]{2,1,0:T(8,128)(2,1)S(1)}, u32[]{:S(2)}, u32[]{:S(2)}) collective-permute-start(bf16[1,384,128]{2,1,0:T(8,128)(2,1)} %get-tuple-element.55), channel_id=1, source_target_pairs={{0,16},{2,18},{4,20},{6,22},{8,24},{10,26},{12,28},{14,30},{16,0},... | collective-permute-start | bytes 294920 | tf_op jit(solution)/shard_map/ppermute | solution.py:28
  158.4 6.6 %collective-permute-start.11 = (bf16[1,384,128]{2,1,0:T(8,128)(2,1)}, bf16[1,384,128]{2,1,0:T(8,128)(2,1)S(1)}, u32[]{:S(2)}, u32[]{:S(2)}) collective-permute-start(bf16[1,384,128]{2,1,0:T(8,128)(2,1)} %get-tuple-element.56), channel_id=1, source_target_pairs={{0,24},{2,26},{4,28},{6,30},{8,16},{10,18},{12,20},{14,22},{16,8},... | collective-permute-start | bytes 294920 | tf_op jit(solution)/shard_map/ppermute | solution.py:28
  160.3 38.5 %collective-permute-start.31 = (bf16[4,384,256]{2,1,0:T(8,128)(2,1)}, bf16[4,384,256]{2,1,0:T(8,128)(2,1)}, u32[]{:S(2)}, u32[]{:S(2)}) collective-permute-start(bf16[4,384,256]{2,1,0:T(8,128)(2,1)} %constant_dynamic-update-slice_fusion.16.refs_4_), channel_id=1, source_target_pairs={{0,2},{2,0},{4,6},{6,4},{8,10},{10,8},{12,14},{14,12},{16,18},{18,... | collective-permute-start | bytes 2359304 | tf_op jit(solution)/shard_map/ppermute | solution.py:28
  165.0 33.9 %collective-permute-start.33 = (bf16[4,384,256]{2,1,0:T(8,128)(2,1)}, bf16[4,384,256]{2,1,0:T(8,128)(2,1)}, u32[]{:S(2)}, u32[]{:S(2)}) collective-permute-start(bf16[4,384,256]{2,1,0:T(8,128)(2,1)} %collective-permute-done.32.refs_6_), channel_id=1, source_target_pairs={{0,2},{2,0},{4,6},{6,4},{8,10},{10,8},{12,14},{14,12},{16,18},{18,... | collective-permute-start | bytes 2359304 | tf_op jit(solution)/shard_map/ppermute | solution.py:28
  165.1 57.9 %collective-permute-start.12 = (bf16[4,384,128]{2,1,0:T(8,128)(2,1)S(1)}, bf16[4,384,128]{2,1,0:T(8,128)(2,1)S(1)}, u32[]{:S(2)}, u32[]{:S(2)}) collective-permute-start(bf16[4,384,128]{2,1,0:T(8,128)(2,1)S(1)} %constant_dynamic-update-slice_fusion.4.refs_0_), channel_id=1, source_target_pairs={{0,1},{1,0},{2,3},{3,2},{4,5},{5,4},{6,7},{7,6},{8,9},{9,8},{10,11... | collective-permute-start | bytes 1179656 | tf_op jit(solution)/shard_map/ppermute | solution.py:28
  177.8 5.9 %collective-permute-start.25 = (bf16[1,384,128]{2,1,0:T(8,128)(2,1)}, bf16[1,384,128]{2,1,0:T(8,128)(2,1)S(1)}, u32[]{:S(2)}, u32[]{:S(2)}) collective-permute-start(bf16[1,384,128]{2,1,0:T(8,128)(2,1)} %get-tuple-element.70), channel_id=1, source_target_pairs={{0,8},{2,10},{4,12},{6,14},{8,0},{10,2},{12,4},{14,6},{16,24},{18,... | collective-permute-start | bytes 294920 | tf_op jit(solution)/shard_map/ppermute | solution.py:28
  183.7 6.9 %collective-permute-start.26 = (bf16[1,384,128]{2,1,0:T(8,128)(2,1)}, bf16[1,384,128]{2,1,0:T(8,128)(2,1)S(1)}, u32[]{:S(2)}, u32[]{:S(2)}) collective-permute-start(bf16[1,384,128]{2,1,0:T(8,128)(2,1)} %get-tuple-element.71), channel_id=1, source_target_pairs={{0,16},{2,18},{4,20},{6,22},{8,24},{10,26},{12,28},{14,30},{16,0},... | collective-permute-start | bytes 294920 | tf_op jit(solution)/shard_map/ppermute | solution.py:28
  190.6 6.6 %collective-permute-start.27 = (bf16[1,384,128]{2,1,0:T(8,128)(2,1)}, bf16[1,384,128]{2,1,0:T(8,128)(2,1)S(1)}, u32[]{:S(2)}, u32[]{:S(2)}) collective-permute-start(bf16[1,384,128]{2,1,0:T(8,128)(2,1)} %get-tuple-element.72), channel_id=1, source_target_pairs={{0,24},{2,26},{4,28},{6,30},{8,16},{10,18},{12,20},{14,22},{16,8},... | collective-permute-start | bytes 294920 | tf_op jit(solution)/shard_map/ppermute | solution.py:28
  197.2 13.7 %copy-start.3 = (bf16[4,384,128]{2,1,0:T(8,128)(2,1)}, bf16[4,384,128]{2,1,0:T(8,128)(2,1)S(1)}, u32[]{:S(2)}) copy-start(bf16[4,384,128]{2,1,0:T(8,128)(2,1)S(1)} %constant_dynamic-update-slice_fusion.12.refs_1_) | copy-start | bytes 1179652
  197.2 33.0 %collective-permute-start.28 = (bf16[4,384,128]{2,1,0:T(8,128)(2,1)S(1)}, bf16[4,384,128]{2,1,0:T(8,128)(2,1)}, u32[]{:S(2)}, u32[]{:S(2)}) collective-permute-start(bf16[4,384,128]{2,1,0:T(8,128)(2,1)S(1)} %constant_dynamic-update-slice_fusion.12.refs_1_), channel_id=1, source_target_pairs={{0,1},{1,0},{2,3},{3,2},{4,5},{5,4},{6,7},{7,6},{8,9},{9,8},{10,11... | collective-permute-start | bytes 1179656 | tf_op jit(solution)/shard_map/ppermute | solution.py:28
  210.9 4.9 %collective-permute-start.34 = (bf16[1,384,128]{2,1,0:T(8,128)(2,1)}, bf16[1,384,128]{2,1,0:T(8,128)(2,1)S(1)}, u32[]{:S(2)}, u32[]{:S(2)}) collective-permute-start(bf16[1,384,128]{2,1,0:T(8,128)(2,1)} %get-tuple-element.77), channel_id=1, source_target_pairs={{0,8},{2,10},{4,12},{6,14},{8,0},{10,2},{12,4},{14,6},{16,24},{18,... | collective-permute-start | bytes 294920 | tf_op jit(solution)/shard_map/ppermute | solution.py:28
  211.0 6.8 %collective-permute-start.35 = (bf16[1,384,128]{2,1,0:T(8,128)(2,1)}, bf16[1,384,128]{2,1,0:T(8,128)(2,1)S(1)}, u32[]{:S(2)}, u32[]{:S(2)}) collective-permute-start(bf16[1,384,128]{2,1,0:T(8,128)(2,1)} %get-tuple-element.78), channel_id=1, source_target_pairs={{0,16},{2,18},{4,20},{6,22},{8,24},{10,26},{12,28},{14,30},{16,0},... | collective-permute-start | bytes 294920 | tf_op jit(solution)/shard_map/ppermute | solution.py:28
  215.8 6.6 %collective-permute-start.36 = (bf16[1,384,128]{2,1,0:T(8,128)(2,1)}, bf16[1,384,128]{2,1,0:T(8,128)(2,1)S(1)}, u32[]{:S(2)}, u32[]{:S(2)}) collective-permute-start(bf16[1,384,128]{2,1,0:T(8,128)(2,1)} %get-tuple-element.79), channel_id=1, source_target_pairs={{0,24},{2,26},{4,28},{6,30},{8,16},{10,18},{12,20},{14,22},{16,8},... | collective-permute-start | bytes 294920 | tf_op jit(solution)/shard_map/ppermute | solution.py:28
  222.5 14.8 %collective-permute-start.37 = (bf16[4,384,128]{2,1,0:T(8,128)(2,1)S(1)}, bf16[4,384,128]{2,1,0:T(8,128)(2,1)}, u32[]{:S(2)}, u32[]{:S(2)}) collective-permute-start(bf16[4,384,128]{2,1,0:T(8,128)(2,1)S(1)} %constant_dynamic-update-slice_fusion.20.refs_1_), channel_id=1, source_target_pairs={{0,1},{1,0},{2,3},{3,2},{4,5},{5,4},{6,7},{7,6},{8,9},{9,8},{10,11... | collective-permute-start | bytes 1179656 | tf_op jit(solution)/shard_map/ppermute | solution.py:28
  (5 other events, 35.4 us)
